TPU v7x, 32 devices: a whole 2x2x4 slice. The times are simulated.
32 devices in a mesh: ens: 2 (over x), tile: 16 (over z, y, core).
Axes of the slice: x: 2, y: 2, z: 4, core: 2. Of those that a mesh axis runs over, the one named last changes fastest.
Arguments:
- fields: bfloat16 [2, 16, 64, 16, 128], P('ens', 'tile'), may hold values from -6 to 6
- cotangent: bfloat16 [2, 16, 64, 16, 128], P('ens', 'tile'), may hold values from -6 to 6
- kernel_first: bfloat16 [9, 64, 64], replicated, may hold values from -0.25 to 0.25
- kernel_second: bfloat16 [9, 128, 64], replicated, may hold values from -0.25 to 0.25
- kernel_third: bfloat16 [9, 128, 128], replicated, may hold values from -0.1875 to 0.1875
- closing_filter_weights: bfloat16 [9, 64, 192], replicated, may hold values from -0.15625 to 0.15625
- offset_first: float32 [64], replicated, may hold values from -3 to 3
- offset_second: float32 [128], replicated, may hold values from -3 to 3
- offset_third: float32 [128], replicated, may hold values from -3 to 3
- closing_shift_values: float32 [64], replicated, may hold values from -3 to 3
- codes: int32 [16, 4], P('tile'), may hold values from 0 to 3
- filter_stride_spread: int32 [4], replicated, may hold values from 1 to 4, as said below
Outputs:
- network_predicted_state: bfloat16 [2, 16, 64, 16, 128], P('ens', 'tile')
- state_input_derivative: float32 [2, 16, 64, 16, 128], P('ens', 'tile')
- initial_filter_derivative: float32 [9, 64, 64], replicated
- latter_filter_derivative: float32 [9, 128, 64], replicated
- penultimate_filter_derivative: float32 [9, 128, 128], replicated
- closing_filter_derivative: float32 [9, 64, 192], replicated
- initial_shift_derivative: float32 [64], replicated
- latter_shift_derivative: float32 [128], replicated
- penultimate_shift_derivative: float32 [128], replicated
- closing_shift_derivative: float32 [64], replicated
Inputs may be any that keep to these rules, and one draw needn't show every extreme that they name: `codes`: bit 0 picks which of the two parallel edges of the sending tile is sent, bit 1 reverses it. `filter_stride_spread`: at least one layer has dilation 4 and one has dilation 1.
All inputs are finite; a program needn't handle non-finite values.
Results may differ from a plain program's by a relative error of at most 0.009.
Values may be sent and summed in bfloat16 or wider, within the bound.
No kernel may reach another device: no remote copies, remote signals or barrier semaphores. Data moves between devices by JAX's collectives and lax.ppermute only.
A program may use at most 128 MiB of HBM per device.

v0:
```python
import functools
import math

import jax
import jax.numpy as jnp
from jax import lax
from jax.experimental import pallas as pl
from jax.experimental.pallas import tpu as pltpu
from jax.sharding import PartitionSpec as P

DMAX = 4
TILE_ROW = 8
LANES = 128
PITCH = 4
F32 = jnp.float32
BF16 = jnp.bfloat16


def lane_of(shape):
    return lax.broadcasted_iota(jnp.int32, shape, len(shape) - 1)


def turn(slab, by):
    if isinstance(by, int):
        by = by % LANES
        if by == 0:
            return slab
    else:
        by = jnp.bitwise_and(by, LANES - 1)
    return pltpu.roll(slab, by, axis=slab.ndim - 1)


def odd(code):
    return jnp.bitwise_and(code, 1)


def flipper(code, width):
    first = lax.broadcasted_iota(jnp.int32, (LANES, LANES), 0)
    second = lax.broadcasted_iota(jnp.int32, (LANES, LANES), 1)
    mirrored = jnp.bitwise_and(width - 1 - first, LANES - 1)
    target = jnp.where(code >= 2, mirrored, first)
    return jnp.where(second == target, 1.0, 0.0).astype(BF16)


def matmul(left, right):
    return jnp.dot(left, right, preferred_element_type=F32)


def matmul_t(left, right):
    return lax.dot_general(left, right, (((1,), (1,)), ((), ())), preferred_element_type=F32)


def halves(values):
    high = values.astype(BF16)
    return high, (values - high.astype(F32)).astype(BF16)


def pack_columns(row, count, first_lane, flip):
    packed = None
    for r in range(count):
        place = r if flip is None else jnp.where(flip, count - 1 - r, r)
        moved = turn(row(r), PITCH * place - first_lane)
        if packed is None:
            packed = moved
        else:
            packed = jnp.where(lane_of(moved.shape) // PITCH == place, moved, packed)
    return packed


def squeeze(packed, used):
    groups = LANES // used
    part = packed.shape[0] // groups
    lane = lane_of((part, LANES))
    whole = packed[:part]
    for g in range(1, groups):
        moved = turn(packed[g * part : (g + 1) * part], used * g)
        whole = jnp.where(lane // used == g, moved, whole)
    return whole


def expand(whole, used):
    groups = LANES // used
    return jnp.concatenate([turn(whole, -used * g) for g in range(groups)], axis=0)


def shorten(packed, count):
    if count <= 8:
        return packed
    return jnp.where(lane_of(packed.shape) < 16, packed, turn(packed, 32 - PITCH * count))


def short_base(code, count, margin):
    return odd(code) * (min(count, 8) - margin)


def units_of(channels, used):
    return channels * used // (LANES * 16)


def put_units(ref, index, at, whole):
    units = whole.shape[0] // 16
    shaped = whole.reshape(units, 16, LANES).astype(BF16)
    if index is None:
        ref[at : at + units] = shaped
    else:
        ref[index, at : at + units] = shaped


def get_units(ref, index, at, channels, used):
    units = units_of(channels, used)
    block = ref[at : at + units] if index is None else ref[index, at : at + units]
    return expand(block.reshape(units * 16, LANES), used)


def by_parity(sc, for_even, for_odd):
    return jnp.where(sc[10] == 0, for_even, for_odd)


def put_sides(refs, index, at, leftward, rightward, sc):
    put_units(refs[0], index, at, by_parity(sc, rightward, leftward))
    put_units(refs[1], index, at, by_parity(sc, leftward, rightward))


def get_sides(refs, index, at, channels, used, sc):
    first = get_units(refs[0], index, at, channels, used)
    second = get_units(refs[1], index, at, channels, used)
    return by_parity(sc, second, first), by_parity(sc, first, second)


def edge_messages(row, ref, sends, places, width, margin, sc):
    count = ref.shape[0]
    row_messages(ref, sends[0], places[0], width, margin, sc)
    packed = []
    for code in (sc[2], sc[3]):
        first_lane = jnp.where(odd(code) == 1, width - margin, 0)
        packed.append(pack_columns(row, count, first_lane, code >= 2))
    near = [squeeze(part, PITCH * count) for part in packed]
    put_sides(sends[1:3], None, places[1], near[0], near[1], sc)
    far = [squeeze(shorten(part, count), 32) for part in packed]
    for index in range(sends[3].shape[0]):
        put_sides(sends[3:5], index, places[2], far[0], far[1], sc)


def pass_on(extras, sends, places):
    for extra, out, at, dim in zip(extras, sends, (places[0],) + (places[1],) * 2 + (places[2],) * 2, (1, 0, 0, 1, 1)):
        size = extra.shape[dim]
        if dim == 0:
            out[at : at + size] = extra[...]
        else:
            for index in range(extra.shape[0]):
                out[index, at : at + size] = extra[index]


def pair_rows(rows, margin):
    half = margin // 2
    lane = lane_of(rows[0].shape)
    return [jnp.where(lane < 64, rows[k], turn(rows[k + half], 64)) for k in range(half)]


def row_messages(ref, out, at, width, margin, sc):
    count, channels = ref.shape[0], ref.shape[1]
    for side in range(2):
        base = jnp.where(odd(sc[side]) == 1, count - margin, 0)
        picked = ref[pl.ds(base, margin)].reshape(margin * channels, LANES).astype(BF16)
        turned = matmul(picked, flipper(sc[side], width)).reshape(margin, channels, LANES)
        store_rows(turned, out, side, at, width, margin)


def store_rows(turned, out, side, at, width, margin):
    channels = turned.shape[1]
    slabs = channels // out.shape[-2]
    rows = [turned[k].astype(BF16) for k in range(margin)]
    if width == 64:
        rows = pair_rows(rows, margin)
    for k, slab in enumerate(rows):
        out[side, at + k * slabs : at + (k + 1) * slabs] = slab.reshape(
            (slabs, channels // slabs, LANES)
        )


def load_row(ref, side, at, k, channels, width, margin):
    slabs = channels // ref.shape[-2]
    half = margin // 2
    index = k % half if width == 64 else k
    slab = ref[side, at + index * slabs : at + (index + 1) * slabs].reshape(channels, LANES)
    return turn(slab, 64) if width == 64 and k >= half else slab


def rim_sides(first, second, base, width, margin, code):
    lane = lane_of(first.shape)
    rows = []
    for k in range(margin):
        left = turn(first, LANES - margin - PITCH * (base + k))
        right = turn(second, width - PITCH * (base + k))
        rows.append(jnp.where(lane >= LANES - margin, left, right))
    channels = first.shape[0]
    flat = jnp.concatenate(rows, axis=0)
    turned = matmul(flat, flipper(code, width)).astype(BF16).reshape(margin, channels, LANES)
    return [turned[k] for k in range(margin)]


def padded_sides(received, places, count, channels, width, margin, sc):
    left, right = get_sides(received[1:3], None, places[1], channels, PITCH * count, sc)
    lane = lane_of((channels, LANES))
    rims = []
    for index, code in ((0, sc[4]), (received[3].shape[0] - 1, sc[5])):
        rims.append(
            rim_sides(
                *get_sides(received[3:5], index, places[2], channels, 32, sc),
                short_base(code, count, margin),
                width,
                margin,
                code,
            )
        )
    center = []
    for r in range(count):
        center.append(
            jnp.where(
                lane >= LANES - margin,
                turn(left, LANES - margin - PITCH * r),
                turn(right, width - PITCH * r),
            )
        )
    return rims[0] + center + rims[1]


def padded_rows(tile, received, places, width, margin, sc):
    rows_in = received[0]
    count, channels = tile.shape[0], tile.shape[1]
    sides = padded_sides(received, places, count, channels, width, margin, sc)
    lane = lane_of((channels, LANES))
    for r in range(count + 2 * margin):
        if r < margin:
            own = load_row(rows_in, 1, places[0], r, channels, width, margin)
        elif r < margin + count:
            own = tile[r - margin]
        else:
            own = load_row(rows_in, 0, places[0], r - margin - count, channels, width, margin)
        if width == 64:
            own = jnp.where(lane < width, own, sides[r])
        yield r, own, sides[r]


def store_shifts(taps, r, at, step, own, sides, width, spacing):
    channels = own.shape[0]
    lane = lane_of(own.shape)
    if width == 64:
        from_left, from_right = own, own
    else:
        from_left = jnp.where(lane >= LANES - spacing, sides, own)
        from_right = jnp.where(lane < spacing, sides, own)
    taps[r, at : at + channels] = turn(from_left, spacing)
    taps[r, step + at : step + at + channels] = own
    taps[r, 2 * step + at : 2 * step + at + channels] = turn(from_right, -spacing)


def fill_taps(taps, tile, received, places, width, sc, spacing):
    channels = tile.shape[1]
    for r, own, sides in padded_rows(tile, received, places, width, DMAX, sc):
        store_shifts(taps, r, 0, channels, own, sides, width, spacing)


def tap_pair(taps, i, spacing):
    sections = []
    for row in (i, i + 1):
        sections.append(
            jnp.concatenate([taps[row + DMAX + (a - 1) * spacing] for a in range(3)], axis=0)
        )
    return jnp.concatenate(sections, axis=1)


def column_of(offset):
    return jnp.concatenate([offset[...], offset[...]], axis=1)


def normal_cdf(values):
    return 0.5 + 0.5 * lax.erf(values * (2.0**-0.5))


def gelu(values):
    return values * normal_cdf(values)


def gelu_slope(values):
    density = jnp.exp(-0.5 * values * values) * (1.0 / math.sqrt(2.0 * math.pi))
    return normal_cdf(values) + values * density


def pool_matrix(weight):
    row = lax.broadcasted_iota(jnp.int32, (2 * LANES, LANES), 0)
    col = lax.broadcasted_iota(jnp.int32, (2 * LANES, LANES), 1)
    return jnp.where(jnp.bitwise_and(row, LANES - 1) // 2 == col, weight, 0.0).astype(BF16)


def side_pool_matrix():
    row = lax.broadcasted_iota(jnp.int32, (2 * LANES, LANES), 0)
    col = lax.broadcasted_iota(jnp.int32, (2 * LANES, LANES), 1)
    row = jnp.bitwise_and(row, LANES - 1)
    target = jnp.where(row >= 124, 126 + (row - 124) // 2, jnp.where(row < 4, 64 + row // 2, -1))
    return jnp.where(target == col, 1.0, 0.0).astype(BF16)


def spread_matrix():
    row = lax.broadcasted_iota(jnp.int32, (LANES, LANES), 0)
    col = lax.broadcasted_iota(jnp.int32, (LANES, LANES), 1)
    return jnp.where(col // 2 == row, 1.0, 0.0).astype(BF16)


def side_spread_matrix():
    row = lax.broadcasted_iota(jnp.int32, (LANES, LANES), 0)
    col = lax.broadcasted_iota(jnp.int32, (LANES, LANES), 1)
    source = jnp.where(col >= 124, 126 + (col - 124) // 2, jnp.where(col < 4, 64 + col // 2, -1))
    return jnp.where(source == row, 1.0, 0.0).astype(BF16)


def fill_delta(delta, rows):
    count = delta.shape[0] - 16
    nothing = jnp.zeros((8,) + delta.shape[1:], BF16)
    delta[0:8] = nothing
    delta[8 + count :] = nothing
    for r in range(count):
        delta[8 + r] = rows(r)


def spread_taps(delta, kernel, spacing, width):
    count = delta.shape[0] - 16
    channels = kernel.shape[0] // 3
    lane = lane_of((channels, LANES))
    for r in range(0, count + 2 * DMAX, 2):
        sections = []
        for row in (r, r + 1):
            sections.append(
                jnp.concatenate(
                    [delta[8 + row - DMAX - (a - 1) * spacing] for a in range(3)], axis=0
                )
            )
        both = matmul(kernel[...], jnp.concatenate(sections, axis=1))
        for k in range(2):
            part = both[:, k * LANES : (k + 1) * LANES]
            to_left = turn(part[:channels], -spacing)
            own = part[channels : 2 * channels]
            to_right = turn(part[2 * channels :], spacing)
            if width == 64:
                own = own + to_left + to_right
                yield r + k, own, own
            else:
                keep_right = lane >= spacing
                keep_left = lane < LANES - spacing
                own = own + jnp.where(keep_right, to_right, 0.0) + jnp.where(keep_left, to_left, 0.0)
                sides = jnp.where(keep_right, 0.0, to_right) + jnp.where(keep_left, 0.0, to_left)
                yield r + k, own, sides


def rim_messages(own, sides, sends, places, width, margin, sc):
    rows_out = sends[0]
    total, channels = own.shape[0], own.shape[1]
    count = total - 2 * margin
    lane = lane_of((channels, LANES))
    near = []
    for first_lane in (-margin, width):
        packed = pack_columns(lambda r: sides[margin + r].astype(BF16), count, first_lane, None)
        near.append(squeeze(packed, PITCH * count))
    put_sides(sends[1:3], None, places[1], near[0], near[1], sc)
    corners = []
    for side, code, start in ((0, sc[4], 0), (1, sc[5], margin + count)):
        mirror = flipper(code, width)
        flat = own[start : start + margin].reshape(margin * channels, LANES).astype(BF16)
        turned = matmul(flat, mirror).reshape(margin, channels, LANES)
        store_rows(turned, rows_out, side, places[0], width, margin)
        if width != 64:
            flat = sides[start : start + margin].reshape(margin * channels, LANES).astype(BF16)
            turned = matmul(flat, mirror).reshape(margin, channels, LANES)
        base = short_base(code, count, margin)
        left = jnp.zeros((channels, LANES), F32)
        right = jnp.zeros((channels, LANES), F32)
        for k in range(margin):
            here = lane // PITCH == base + k
            left = jnp.where(here, turn(turned[k], PITCH * (base + k) + margin), left)
            right = jnp.where(here, turn(turned[k], PITCH * (base + k) - width), right)
        corners.append((squeeze(left, 32), squeeze(right, 32)))
    if sends[3].shape[0] == 1:
        both = [corners[0][i] + corners[1][i] for i in range(2)]
        put_sides(sends[3:5], 0, places[2], both[0], both[1], sc)
    else:
        for index in range(2):
            left, right = corners[1 - index]
            put_sides(sends[3:5], index, places[2], left, right, sc)


def fold(total, inner, received, places, width, margin, sc):
    rows_in = received[0]
    count, channels = inner.shape[0], inner.shape[1]
    lane = lane_of((channels, LANES))
    used = PITCH * count
    found = [
        side.astype(F32)
        for side in get_sides(received[1:3], None, places[1], channels, used, sc)
    ]
    for index in range(received[3].shape[0]):
        for i, short in enumerate(get_sides(received[3:5], index, places[2], channels, 32, sc)):
            short = short.astype(F32)
            if count <= 8:
                found[i] = found[i] + jnp.where(lane < 32, short, 0.0)
            else:
                late = turn(short, used - 32)
                late = jnp.where((lane >= used - 16) & (lane < used), late, 0.0)
                found[i] = found[i] + jnp.where(lane < 16, short, late)
    for r in range(count):
        row = inner[r]
        for packed, code in ((found[0], sc[2]), (found[1], sc[3])):
            first = jnp.where(odd(code) == 1, width - margin, 0)
            place = jnp.where(code >= 2, count - 1 - r, r)
            moved = turn(packed, first - PITCH * place)
            row = row + jnp.where((lane >= first) & (lane < first + margin), moved, 0.0)
        total[r] = row
    for side, code in ((0, sc[1]), (1, sc[0])):
        base = odd(code) * (count - margin)
        for k in range(margin):
            total[base + k] = total[base + k] + load_row(
                rows_in, side, places[0], k, channels, width, margin
            ).astype(F32)


START = (0, 0, 0)
AFTER_POOLED = (2, 1, 1)
AFTER_SECOND = (4, 2, 2)


def weights_kernel(swapped, *refs):
    kernels, arrived = refs[20:24], refs[24]
    copies = [pltpu.make_async_copy(refs[i], kernels[i], arrived.at[i]) for i in range(4)]
    for copy in copies:
        copy.start()
    for i, (kernel, offset) in enumerate(zip(kernels, refs[4:8])):
        forward, backward, shift = refs[8 + i], refs[12 + i], refs[16 + i]
        copies[i].wait()
        outs, channels = kernel.shape[1:]
        if swapped[i]:
            outs, channels = channels, outs
        for tap in range(9):
            a, e = tap // 3, tap % 3
            own = kernel[tap]
            across = jnp.transpose(own.astype(F32)).astype(BF16)
            if swapped[i]:
                own, across = across, own
            forward[:, tap * channels : (tap + 1) * channels] = own
            backward[e * channels : (e + 1) * channels, a * outs : (a + 1) * outs] = across
        row = lax.broadcasted_iota(jnp.int32, (outs, outs), 0)
        col = lax.broadcasted_iota(jnp.int32, (outs, outs), 1)
        column = jnp.sum(jnp.where(row == col, offset[...], 0.0), axis=1, keepdims=True)
        shift[...] = jnp.broadcast_to(column, shift.shape)


def fields_kernel(sc, fields, tile, *sends):
    tile[...] = jnp.swapaxes(fields[...], 0, 1)
    edge_messages(lambda r: tile[r], tile, sends, START, LANES, DMAX, sc)
    last, shape = sends[0].shape[1] - 1, sends[0].shape[2:]
    for side in range(2):
        code = sc[side].astype(F32)
        sends[0][side, last] = jnp.broadcast_to(code, shape).astype(BF16)


def first_kernel(own_sc, tile, *refs):
    received, (kernel, offset) = refs[:5], refs[5:7]
    act_out, pre_out, pooled_out, sc, taps = refs[7:12]
    sends = refs[12:]
    last = received[0].shape[1] - 1
    for i in range(13):
        sc[i] = own_sc[i]
    for i in range(2):
        sc[4 + i] = jnp.max(received[0][1 - i, last].astype(F32)).astype(jnp.int32)
    spacing = own_sc[6]
    fill_taps(taps, tile, received, START, LANES, sc, spacing)
    pool = pool_matrix(0.25)
    shift = column_of(offset)
    for i in range(0, tile.shape[0], 2):
        pre = matmul(kernel[...], tap_pair(taps, i, spacing)) + shift
        act = gelu(pre).astype(BF16)
        for k in range(2):
            act_out[i + k] = act[:, k * LANES : (k + 1) * LANES]
            pre_out[i + k] = pre[:, k * LANES : (k + 1) * LANES]
        pooled_out[i // 2] = matmul(act, pool).astype(BF16)
    edge_messages(
        lambda r: pooled_out[r], pooled_out, sends, START, 64, DMAX, sc
    )
    edge_messages(
        lambda r: act_out[r], act_out, sends, AFTER_POOLED, LANES, DMAX, sc
    )


def second_kernel(sc, tile, *refs):
    received, (kernel, offset), extras = refs[:5], refs[5:7], refs[7:12]
    act_out, pre_out, taps = refs[12:15]
    sends = refs[15:]
    spacing = sc[7]
    fill_taps(taps, tile, received, START, 64, sc, spacing)
    shift = column_of(offset)
    for i in range(0, tile.shape[0], 2):
        pre = matmul(kernel[...], tap_pair(taps, i, spacing)) + shift
        both = beside(pre[:, :LANES], pre[:, LANES:])
        act = gelu(both).astype(BF16)
        for k in range(2):
            act_out[i + k] = turn(act, 64 * k)
        pre_out[i // 2] = both
    edge_messages(lambda r: act_out[r], act_out, sends, START, 64, DMAX, sc)
    pass_on(extras, sends, AFTER_SECOND)


def slopes_kernel(*refs):
    half = len(refs) // 2
    for values, out in zip(refs[:half], refs[half:]):
        for r in range(values.shape[0]):
            out[r] = gelu_slope(values[r])


def beside(first, second):
    return jnp.where(lane_of(first.shape) < 64, first, turn(second, 64))


def masked(values, width):
    return jnp.where(lane_of(values.shape) < width, values, jnp.zeros_like(values))


def back_part(sc, delta, kernel, spacing, width, inner_out, sends, own_all, sides_all):
    count = delta.shape[0] - 16
    for r, own, sides in spread_taps(delta, kernel, spacing, width):
        own_all[r] = own
        if width != 64:
            sides_all[r] = sides
    for r in range(count):
        inner_out[r] = own_all[DMAX + r]
    rim_messages(own_all, sides_all, sends, START, width, DMAX, sc)


def third_kernel(sc, tile, *refs):
    received, (kernel, offset, coarse, back) = refs[:5], refs[5:9]
    act_out, delta_out, inner_out = refs[9:12]
    sends, (taps, delta, own_all, coarse_sum) = refs[12:17], refs[17:]
    fold(coarse_sum, coarse, received, AFTER_SECOND, 64, 2, sc)
    spacing = sc[8]
    fill_taps(taps, tile, received, START, 64, sc, spacing)
    shift = column_of(offset)
    for i in range(0, tile.shape[0], 2):
        pre = matmul(kernel[...], tap_pair(taps, i, spacing)) + shift
        both = beside(pre[:, :LANES], pre[:, LANES:])
        act = gelu(both).astype(BF16)
        change = (beside(coarse_sum[i], coarse_sum[i + 1]) * gelu_slope(both)).astype(BF16)
        for k in range(2):
            act_out[i + k] = turn(act, 64 * k)
            delta_out[i + k] = masked(turn(change, 64 * k), 64)
    fill_delta(delta, lambda r: delta_out[r])
    back_part(sc, delta, back, spacing, 64, inner_out, sends, own_all, own_all)
    edge_messages(lambda r: act_out[r], act_out, sends, AFTER_SECOND, 64, 2, sc)


def middle_kernel(sc, inner, *refs):
    received, (slope, back), extras = refs[:5], refs[5:7], refs[7:12]
    delta_out, inner_out = refs[12:14]
    sends, (total, delta, own_all) = refs[14:19], refs[19:]
    fold(total, inner, received, START, 64, DMAX, sc)
    for r in range(0, inner.shape[0], 2):
        change = (beside(total[r], total[r + 1]) * slope[r // 2]).astype(BF16)
        for k in range(2):
            delta_out[r + k] = masked(turn(change, 64 * k), 64)
    fill_delta(delta, lambda r: delta_out[r])
    back_part(sc, delta, back, sc[7], 64, inner_out, sends, own_all, own_all)
    pass_on(extras, sends, AFTER_POOLED)


def lower_kernel(sc, inner, *refs):
    received, (slope, skip_inner, back) = refs[:5], refs[5:8]
    delta_out, inner_out = refs[8:10]
    sends, (total, skip, delta, own_all, sides_all) = refs[10:15], refs[15:]
    fold(total, inner, received, START, 64, DMAX, sc)
    fold(skip, skip_inner, received, AFTER_POOLED, LANES, DMAX, sc)
    spread = spread_matrix()
    for r in range(inner.shape[0]):
        lane = lane_of(total[r].shape)
        high, low = halves(jnp.where(lane < 64, total[r], 0.0))
        wide = 0.25 * (matmul(high, spread) + matmul(low, spread))
        for k in range(2):
            row = 2 * r + k
            delta_out[row] = ((skip[row] + wide) * slope[row]).astype(BF16)
    fill_delta(delta, lambda r: delta_out[r])
    back_part(sc, delta, back, sc[6], LANES, inner_out, sends, own_all, sides_all)


def last_kernel(sc, inner, *refs):
    received, out, total = refs[:5], refs[5], refs[6]
    fold(total, inner, received, START, LANES, DMAX, sc)
    out[...] = jnp.swapaxes(total[...], 0, 1)


def upstream_kernel(sc, cotangent, back, *refs):
    upstream, coarse_out, skip_out = refs[:3]
    coarse_sends, skip_sends = refs[3:8], refs[8:13]
    delta, own_all, sides_all, coarse_all = refs[13:]
    upstream[...] = jnp.swapaxes(cotangent[...], 0, 1)
    fill_delta(delta, lambda r: upstream[r])
    pool = jnp.concatenate([pool_matrix(1.0), side_pool_matrix()], axis=0)
    pending = None
    for r, own, sides in spread_taps(delta, back, sc[9], LANES):
        own_all[r] = own[128:]
        sides_all[r] = sides[128:]
        if pending is None:
            pending = (own[:128], sides[:128])
        else:
            high, low = halves(
                jnp.concatenate([pending[0], own[:128], pending[1], sides[:128]], axis=1)
            )
            coarse_all[r // 2] = matmul(high, pool) + matmul(low, pool)
            pending = None
    for r in range(coarse_out.shape[0]):
        coarse_out[r] = coarse_all[2 + r]
    for r in range(skip_out.shape[0]):
        skip_out[r] = own_all[4 + r]
    rim_messages(coarse_all, coarse_all, coarse_sends, START, 64, 2, sc)
    rim_messages(own_all, sides_all, skip_sends, START, LANES, 4, sc)


def put_terms(out, at, sums, sides):
    outs, columns = sums.shape
    whole = columns // LANES
    for k in range(whole):
        out[at + k * outs : at + (k + 1) * outs] = sums[:, k * LANES : (k + 1) * LANES].astype(BF16)
    if columns % LANES:
        wide = jnp.concatenate(
            [jnp.broadcast_to(side, (outs, 64 // len(sides))) for side in sides], axis=1
        )
        tail = jnp.concatenate([sums[:, whole * LANES :], wide], axis=1)
        out[at + whole * outs : at + (whole + 1) * outs] = tail.astype(BF16)


def row_sum(rows):
    total = None
    for r in range(rows.shape[0]):
        row = rows[r].astype(F32)
        total = row if total is None else total + row
    return jnp.sum(total, axis=1, keepdims=True)


def layer_terms(taps, delta, spacing, use=None):
    sums = None
    for i in range(0, delta.shape[0], 2):
        section = tap_pair(taps, i, spacing)
        if use is not None:
            use(i, section)
        part = matmul_t(jnp.concatenate([delta[i], delta[i + 1]], axis=1), section)
        sums = part if sums is None else sums + part
    return sums


def third_terms_kernel(sc, second, delta, *refs):
    third_in, (out, taps) = refs[:5], refs[5:]
    fill_taps(taps, second, third_in, START, 64, sc, sc[8])
    put_terms(out, 0, layer_terms(taps, delta, sc[8]), None)


def joined_kernel(
    sc, coarse, fine, taps_second, delta_third, delta_second, upstream, kernel, offset, *refs
):
    second_in, back_in = refs[:5], refs[5:10]
    state_out, out, taps, state_all = refs[10:]
    sums = layer_terms(taps_second, delta_second, sc[7])
    put_terms(out, 0, sums, [row_sum(delta_second), row_sum(delta_third)])
    after = -(-sums.shape[1] // LANES) * sums.shape[0]
    spacing = sc[9]
    spread = jnp.concatenate([spread_matrix(), side_spread_matrix()], axis=1)
    for r, own, _ in padded_rows(coarse, back_in, AFTER_SECOND, 64, 2, sc):
        wide = matmul(own, spread).astype(BF16)
        for k in range(2):
            store_shifts(
                taps, 2 * r + k, 0, 192, wide[:, :LANES], wide[:, LANES:], LANES, spacing
            )
    for r, own, sides in padded_rows(fine, second_in, AFTER_POOLED, LANES, 4, sc):
        store_shifts(taps, r, 128, 192, own, sides, LANES, spacing)
    shift = column_of(offset)

    def use(i, section):
        state = (matmul(kernel[...], section) + shift).astype(BF16)
        for k in range(2):
            state_all[i + k] = state[:, k * LANES : (k + 1) * LANES]

    put_terms(out, after, layer_terms(taps, upstream, spacing, use), [row_sum(upstream)])
    state_out[...] = jnp.swapaxes(state_all[...], 0, 1)


def first_terms_kernel(sc, taps, delta, third_terms, terms, give, keep, whole):
    rows = 0
    for part in (third_terms, terms):
        whole[rows : rows + part.shape[0]] = part[...]
        rows += part.shape[0]
    sums = layer_terms(taps, delta, sc[6])
    put_terms(whole, rows, sums, [row_sum(delta)])
    rows += -(-sums.shape[1] // LANES) * sums.shape[0]
    whole[rows:] = jnp.zeros((whole.shape[0] - rows, LANES), BF16)
    half = keep.shape[0]
    keep[...] = whole[pl.ds(pl.multiple_of(sc[10] * half, 16), half)]
    give[...] = whole[pl.ds(pl.multiple_of((1 - sc[10]) * half, 16), half)]


def core_sum_kernel(sc, keep, given, own, *gives):
    size = own.shape[0]
    for i, out in enumerate((own,) + gives):
        member = sc[11] if i < 2 else 1 - sc[11]
        chip = sc[12] if i % 2 == 0 else 1 - sc[12]
        rows = pl.ds(pl.multiple_of((2 * member + chip) * size, 16), size)
        out[...] = (keep[rows].astype(F32) + given[rows].astype(F32)).astype(out.dtype)


def adding_kernel(*refs):
    total = refs[0][...].astype(F32)
    for ref in refs[1:-1]:
        total = total + ref[...].astype(F32)
    refs[-1][...] = total.astype(BF16)


def unpack_kernel(scale, layouts, biases, sc, *refs):
    eighths, outs, summed = refs[:8], refs[8:-1], refs[-1]
    size = eighths[0].shape[0]
    for i, eighth in enumerate(eighths):
        bits = [sc[10 + k] if (i >> (2 - k)) % 2 == 0 else 1 - sc[10 + k] for k in range(3)]
        at = pl.multiple_of((4 * bits[0] + 2 * bits[1] + bits[2]) * size, 16)
        summed[pl.ds(at, size)] = eighth[...]
    for (start, outs_count, channels, swapped), out in zip(layouts, outs):
        def slab_at(slab):
            first = start + slab * outs_count
            return summed[first : first + outs_count].astype(F32) * scale

        if swapped:
            for slab in range(5):
                across = jnp.transpose(slab_at(slab))
                for tap in range(2 * slab, min(2 * slab + 2, 9)):
                    at = (tap - 2 * slab) * channels
                    out[tap] = across[at : at + channels]
            continue
        for tap in range(9):
            first, last = tap * channels, (tap + 1) * channels
            found = []
            while first < last:
                slab = first // LANES
                end = min(last, (slab + 1) * LANES)
                found.append(slab_at(slab)[:, first - slab * LANES : end - slab * LANES])
                first = end
            out[tap] = found[0] if len(found) == 1 else jnp.concatenate(found, axis=1)
    for (start, count, lane), out in zip(biases, outs[len(layouts) :]):
        block = summed[start : start + count].astype(F32)
        column = jnp.sum(
            jnp.where(lane_of(block.shape) == lane, block, 0.0), axis=1, keepdims=True
        )
        row = lax.broadcasted_iota(jnp.int32, (count, count), 0)
        col = lax.broadcasted_iota(jnp.int32, (count, count), 1)
        out[...] = jnp.sum(jnp.where(row == col, column, 0.0), axis=0, keepdims=True) * scale


def call(body, inputs, outputs, scratch=(), flops=0, scalars=1, copied=0, name=None):
    specs = [pl.BlockSpec(memory_space=pltpu.VMEM)] * len(inputs)
    specs[:copied] = [pl.BlockSpec(memory_space=pl.ANY)] * copied
    arrived = [pltpu.SemaphoreType.DMA((copied,))] if copied else []
    for i in range(scalars):
        specs[i] = pl.BlockSpec(memory_space=pltpu.SMEM)
    moved = sum(math.prod(shape) * jnp.dtype(kind).itemsize for shape, kind in outputs)
    moved += sum(array.size * array.dtype.itemsize for array in inputs)
    spaces = [pltpu.SMEM if kind == jnp.int32 else pltpu.VMEM for _, kind in outputs]
    return pl.pallas_call(
        body,
        out_shape=[jax.ShapeDtypeStruct(shape, kind) for shape, kind in outputs],
        in_specs=specs,
        out_specs=[pl.BlockSpec(memory_space=space) for space in spaces],
        scratch_shapes=[pltpu.VMEM(shape, kind) for shape, kind in scratch] + arrived,
        compiler_params=pltpu.CompilerParams(vmem_limit_bytes=24 * 1024 * 1024),
        cost_estimate=pl.CostEstimate(flops=flops, bytes_accessed=moved, transcendentals=0),
        name=name,
    )(*inputs)


def shifted(array, for_even, for_odd):
    devices = lax.axis_size("tile")
    pairs = [(i, (i + (for_odd if i % 2 else for_even)) % devices) for i in range(devices)]
    return lax.ppermute(array, "tile", pairs)


def wrapped():
    return lax.axis_size("tile") == 2 * TILE_ROW


def other_tile(array, bit):
    pairs = [(i, i ^ (1 << bit)) for i in range(lax.axis_size("tile"))]
    return lax.ppermute(array, "tile", pairs)


def other_member(array):
    return lax.ppermute(array, "ens", [(0, 1), (1, 0)])


def other_both(array, bit):
    tiles = lax.axis_size("tile")
    pairs = [(i, (i ^ (1 << bit)) + tiles if i < tiles else (i ^ (1 << bit)) - tiles)
             for i in range(2 * tiles)]
    return lax.ppermute(array, ("ens", "tile"), pairs)


def exchange_rows(rows):
    if wrapped():
        return shifted(rows, TILE_ROW, TILE_ROW)
    return jnp.stack(
        [shifted(rows[0], -TILE_ROW, -TILE_ROW), shifted(rows[1], TILE_ROW, TILE_ROW)]
    )


def exchange(rows, near_a, near_b, far_a, far_b):
    row = TILE_ROW
    rows_in = exchange_rows(rows)
    if wrapped():
        a_in = shifted(far_a, row + 1, row - 1)
        b_in = shifted(far_b, row - 1, row + 1)
    else:
        a_in = jnp.stack(
            [shifted(far_a[0], row + 1, row - 1), shifted(far_a[1], 1 - row, -1 - row)]
        )
        b_in = jnp.stack(
            [shifted(far_b[0], row - 1, row + 1), shifted(far_b[1], -1 - row, 1 - row)]
        )
    return [rows_in, shifted(near_a, 1, -1), shifted(near_b, -1, 1), a_in, b_in]


def shards(
    fields,
    cotangent,
    kernel_first,
    kernel_second,
    kernel_third,
    closing_filter_weights,
    offset_first,
    offset_second,
    offset_third,
    closing_shift_values,
    codes,
    filter_stride_spread,
):
    members, _, low, height, width = fields.shape
    high = kernel_third.shape[1]
    half = height // 2
    fars = 1 if wrapped() else 2
    tile_index = lax.axis_index("tile")
    place = [tile_index & 1, lax.axis_index("ens") & 1, (tile_index >> 1) & 1]
    own_sc = jnp.concatenate(
        [codes[0], jnp.zeros((2,), jnp.int32), filter_stride_spread]
        + [bit.astype(jnp.int32)[None] for bit in place]
    )

    def sends(rows, near, far):
        return (
            [((2, rows, 64, LANES), BF16)]
            + [((near, 16, LANES), BF16)] * 2
            + [((fars, far, 16, LANES), BF16)] * 2
        )

    fine_tile = ((height, low, LANES), BF16)
    fine_grad = ((height, low, LANES), F32)
    tile, *sent = call(
        fields_kernel,
        [own_sc, fields[0, 0]],
        [fine_tile, ((2, DMAX * low // 16 + 1, 16, LANES), BF16)] + sends(5, 2, 1)[1:],
        name="fields_edges",
    )
    first_in = exchange(*sent)

    weights = [kernel_first, kernel_second, kernel_third, closing_filter_weights]
    offsets = [offset_first, offset_second, offset_third, closing_shift_values]
    swapped = [k.shape[1] % LANES == 0 and k.shape[2] % LANES != 0 for k in weights]
    forms = call(
        functools.partial(weights_kernel, swapped),
        [jnp.swapaxes(k, 1, 2) if swap else k for k, swap in zip(weights, swapped)]
        + [offset[None] for offset in offsets],
        scratch=[
            ((9, k.shape[2], k.shape[1]) if swap else k.shape, BF16)
            for k, swap in zip(weights, swapped)
        ],
        copied=4,
        outputs=        [((k.shape[1], 9 * k.shape[2]), BF16) for k in weights]
        + [((3 * k.shape[2], 3 * k.shape[1]), BF16) for k in weights]
        + [((k.shape[1], LANES), F32) for k in weights],
        scalars=0,
        name="weights",
    )
    forward, backward, shifts = forms[:4], forms[4:8], forms[8:]

    first_taps = ((height + 8, 3 * low, LANES), BF16)
    act_first, pre_first, pooled, sc, taps_first, *sent = call(
        first_kernel,
        [own_sc, tile, *first_in, forward[0], shifts[0]],
        [fine_tile, fine_grad, ((half, low, LANES), BF16), ((13,), jnp.int32), first_taps]
        + sends(6, 3, 2),
        flops=2 * 9 * low * low * height * width,
        name="first_layer",
    )
    second_in = exchange(*sent)

    upstream, coarse_inner, skip_inner, *rims = call(
        upstream_kernel,
        [sc, cotangent[0, 0], backward[3]],
        [fine_tile, ((half, high, LANES), F32), fine_grad] + sends(2, 2, 2) + sends(4, 2, 1),
        [
            ((height + 16, low, LANES), BF16),
            ((height + 8, low, LANES), F32),
            ((height + 8, low, LANES), F32),
            ((half + 4, high, LANES), F32),
        ],
        flops=2 * 9 * low * (low + high) * height * width,
        name="cotangent_back",
    )
    coarse_rims, skip_rims = rims[:5], rims[5:]

    second_taps = ((half + 8, 3 * low, LANES), BF16)
    act_second, pre_second, taps_second, *sent = call(
        second_kernel,
        [sc, pooled, *second_in, forward[1], shifts[1], *coarse_rims],
        [((half, high, LANES), BF16), ((half // 2, high, LANES), F32), second_taps]
        + sends(6, 4, 4),
        flops=2 * 9 * low * high * half * LANES,
        name="second_layer",
    )
    third_in = exchange(*sent)
    slope_first, slope_second = call(
        slopes_kernel,
        [pre_first, pre_second],
        [fine_grad, ((half // 2, high, LANES), F32)],
        scalars=0,
        name="slopes",
    )
    coarse_inner, slope_first = lax.optimization_barrier((coarse_inner, slope_first))

    third_taps = ((half + 8, 3 * high, LANES), BF16)
    act_third, delta_third, inner, *sent = call(
        third_kernel,
        [sc, act_second, *third_in, forward[2], shifts[2], coarse_inner, backward[2]],
        [((half, high, LANES), BF16)] * 2 + [((half, high, LANES), F32)] + sends(6, 4, 4),
        [
            third_taps,
            ((half + 16, high, LANES), BF16),
            ((half + 8, high, LANES), F32),
            ((half, high, LANES), F32),
        ],
        flops=2 * 2 * 9 * high * high * half * LANES,
        name="third_layer_and_back",
    )
    back_in = exchange(*sent)
    (third_terms,) = call(
        third_terms_kernel,
        [sc, act_second, delta_third, *third_in],
        [((9 * high, LANES), BF16)],
        [third_taps],
        flops=2 * 9 * high * high * half * LANES,
        name="third_terms",
    )
    inner, third_terms = lax.optimization_barrier((inner, third_terms))

    delta_second, inner, *sent = call(
        middle_kernel,
        [sc, inner, *back_in, slope_second, backward[1], *skip_rims],
        [((half, high, LANES), BF16), ((half, low, LANES), F32)] + sends(6, 3, 2),
        [
            ((half, high, LANES), F32),
            ((half + 16, high, LANES), BF16),
            ((half + 8, low, LANES), F32),
        ],
        flops=2 * 9 * low * high * half * LANES,
        name="second_back",
    )
    lower_in = exchange(*sent)

    narrow = -(-9 * low // LANES)
    wide = -(-9 * (low + high) // LANES)
    upper_rows = narrow * high + wide * low
    state, upper_terms = call(
        joined_kernel,
        [
            sc, act_third, act_first, taps_second, delta_third, delta_second, upstream, forward[3],
            shifts[3], *second_in, *back_in,
        ],
        [((low, height, LANES), BF16), ((upper_rows, LANES), BF16)],
        [
            ((height + 8, 3 * (low + high), LANES), BF16),
            fine_tile,
        ],
        flops=2 * 2 * 9 * low * (low + high) * height * width,
        name="joined_layer_and_terms",
    )
    lower_in[0], upper_terms = lax.optimization_barrier((lower_in[0], upper_terms))

    delta_first, inner, *sent = call(
        lower_kernel,
        [sc, inner, *lower_in, slope_first, skip_inner, backward[0]],
        [fine_tile, fine_grad] + sends(4, 2, 1),
        [
            ((half, low, LANES), F32),
            fine_grad,
            ((height + 16, low, LANES), BF16),
            ((height + 8, low, LANES), F32),
            ((height + 8, low, LANES), F32),
        ],
        flops=2 * 9 * low * low * height * width,
        name="first_back",
    )

    tiles = lax.axis_size("tile")
    rows = 9 * high + upper_rows + narrow * low
    size = -(-rows // (8 * 16)) * 16

    def part(count):
        return ((count * size, LANES), BF16)

    give, keep = call(
        first_terms_kernel,
        [sc, taps_first, delta_first, third_terms, upper_terms],
        [part(4)] * 2,
        [part(8)],
        flops=2 * 9 * low * low * height * width,
        name="first_terms",
    )
    given = other_tile(give, 0)
    own, *gives = call(
        core_sum_kernel,
        [sc, keep, given],
        [((size, LANES), F32)] + [part(1)] * 3,
        name="core_sum",
    )
    given = [other_tile(gives[0], 1), other_member(gives[1]), other_both(gives[2], 1)]
    last_in = exchange(*sent)
    (total,) = call(adding_kernel, [own, *given], [part(1)], scalars=0, name="chip_sum")
    last_bit = tiles.bit_length() - 2
    for bit in range(2, last_bit + 1):
        if bit == last_bit:
            total, *last_in = lax.optimization_barrier((total, *last_in))
        given = other_tile(total, bit)
        (total,) = call(adding_kernel, [total, given], [part(1)], scalars=0, name=f"sum_{bit}")
    (derivative,) = call(
        last_kernel,
        [sc, inner, *last_in],
        [((low, height, LANES), F32)],
        [fine_grad],
        name="last_fold",
    )

    total, derivative = lax.optimization_barrier((total, derivative))
    eighths = [total, other_tile(total, 1), other_member(total), other_both(total, 1)]
    eighths = eighths + [other_tile(eighth, 0) for eighth in eighths]

    all_tiles = members * lax.axis_size("ens") * lax.axis_size("tile")
    scale = 1.0 / math.sqrt(all_tiles * height * width)
    upper_rows += 9 * high
    starts = [upper_rows, 9 * high, 0, upper_rows - wide * low]
    layouts = [
        (start, k.shape[1], k.shape[2], swap) for start, k, swap in zip(starts, weights, swapped)
    ]
    tail = 9 * high + (narrow - 1) * high
    biases = [(rows - low, low, 64), (tail, high, 64), (tail, high, 96), (upper_rows - low, low, 64)]
    grads = call(
        functools.partial(unpack_kernel, scale, layouts, biases),
        [sc, *eighths],
        [
            ((9, channels, outs) if swap else (9, outs, channels), F32)
            for _, outs, channels, swap in layouts
        ]
        + [((1, count), F32) for _, count, _ in biases],
        [part(8)],
        name="unpack_sums",
    )
    return (
        state[None, None],
        derivative[None, None],
        *[jnp.swapaxes(g, 1, 2) if swap else g for g, swap in zip(grads[:4], swapped)],
        *[grad[0] for grad in grads[4:]],
    )


def solution(mesh):
    tiles = P("ens", "tile", None, None, None)
    in_specs = (tiles, tiles) + (P(),) * 8 + (P("tile", None), P())
    out_specs = (tiles, tiles) + (P(),) * 8
    return jax.shard_map(shards, mesh=mesh, in_specs=in_specs, out_specs=out_specs, check_vma=False)
```

profile of v0, /device:TPU:0, one launch (start us, length us, event | category | flops | bytes accessed | tf_op | source)
XLA Modules:
  0.0 128.1 jit_solution(11561741634957471167)
XLA Ops:
  3.3 4.1 %collective-permute-start = (bf16[2,17,16,128]{3,2,1,0:T(8,128)(2,1)S(1)}, bf16[2,17,16,128]{3,2,1,0:T(8,128)(2,1)S(1)}, u32[]{:S(2)}, u32[]{:S(2)}) collective-permute-start(bf16[2,17,16,128]{3,2,1,0:T(8,128)(2,1)S(1)} %get-tuple-element.114), channel_id=1, source_target_pairs={{0,8},{1,9},{2,10},{3,11},{4,12},{5,13},{6,14},{7,15},{8,0},{9,1},... | collective-permute-start | bytes 417800 | tf_op jit(solution)/shard_map/ppermute | solution.py:781
  7.4 2.4 %collective-permute-start.2 = (bf16[2,16,128]{2,1,0:T(8,128)(2,1)S(1)}, bf16[2,16,128]{2,1,0:T(8,128)(2,1)S(1)}, u32[]{:S(2)}, u32[]{:S(2)}) collective-permute-start(bf16[2,16,128]{2,1,0:T(8,128)(2,1)S(1)} %get-tuple-element.116), channel_id=1, source_target_pairs={{0,15},{1,2},{2,1},{3,4},{4,3},{5,6},{6,5},{7,8},{8,7},{9,10},{10,... | collective-permute-start | bytes 24584 | tf_op jit(solution)/shard_map/ppermute | solution.py:781
  18.7 3.8 %first_layer.1 = (bf16[16,64,128]{2,1,0:T(8,128)(2,1)S(1)}, f32[16,64,128]{2,1,0:T(8,128)S(1)}, bf16[8,64,128]{2,1,0:T(8,128)(2,1)S(1)}, s32[13]{0:T(128)S(1)}, ...) custom-call(s32[13]{0:T(128)S(1)} %concatenate.3.sc.own_sc, ...), custom_call_target="tpu_custom_call" | custom-call | flops 150994944 | bytes 2867304 | tf_op jit(solution)/shard_map/first_layer/pallas_call | solution.py:766
  22.6 2.7 %collective-permute-start.5 = (bf16[2,6,64,128]{3,2,1,0:T(8,128)(2,1)S(1)}, bf16[2,6,64,128]{3,2,1,0:T(8,128)(2,1)S(1)}, u32[]{:S(2)}, u32[]{:S(2)}) collective-permute-start(bf16[2,6,64,128]{3,2,1,0:T(8,128)(2,1)S(1)} %get-tuple-element.123), channel_id=1, source_target_pairs={{0,8},{1,9},{2,10},{3,11},{4,12},{5,13},{6,14},{7,15},{8,0},{9,1},... | collective-permute-start | bytes 589832 | tf_op jit(solution)/shard_map/ppermute | solution.py:781
  30.2 6.3 %cotangent_back.1 = (bf16[16,64,128]{2,1,0:T(8,128)(2,1)S(1)}, f32[8,128,128]{2,1,0:T(8,128)S(1)}, f32[16,64,128]{2,1,0:T(8,128)S(1)}, bf16[2,2,64,128]{3,2,1,0:...) custom-call(s32[13]{0:T(128)S(1)} %get-tuple-element.121.sc, ...), custom_call_target="tpu_custom_call" | custom-call | flops 452984832 | bytes 2048052 | tf_op jit(solution)/shard_map/cotangent_back/pallas_call | solution.py:766
  36.6 1.9 %second_layer.1 = (bf16[8,128,128]{2,1,0:T(8,128)(2,1)S(1)}, f32[4,128,128]{2,1,0:T(8,128)S(1)}, bf16[16,192,128]{2,1,0:T(8,128)(2,1)S(1)}, bf16[2,6,64,128]{3,2...) custom-call(s32[13]{0:T(128)S(1)} %get-tuple-element.121.sc, ...), custom_call_target="tpu_custom_call" | custom-call | flops 150994944 | bytes 2252852 | tf_op jit(solution)/shard_map/second_layer/pallas_call | solution.py:766
  39.5 3.2 %collective-permute-start.12 = (bf16[4,16,128]{2,1,0:T(8,128)(2,1)S(1)}, bf16[4,16,128]{2,1,0:T(8,128)(2,1)S(1)}, u32[]{:S(2)}, u32[]{:S(2)}) collective-permute-start(bf16[4,16,128]{2,1,0:T(8,128)(2,1)S(1)} %get-tuple-element.139), channel_id=1, source_target_pairs={{0,15},{1,2},{2,1},{3,4},{4,3},{5,6},{6,5},{7,8},{8,7},{9,10},{10,... | collective-permute-start | bytes 49160 | tf_op jit(solution)/shard_map/ppermute | solution.py:781
  44.7 3.5 %collective-permute-done.12.refs_2_ = bf16[4,16,128]{2,1,0:T(8,128)(2,1)S(1)} collective-permute-done((bf16[4,16,128]{2,1,0:T(8,128)(2,1)S(1)}, bf16[4,16,128]{2,1,0:T(8,128)(2,1)S(1)}, u32[]{:S(2)}, u32[]{:S(2)}) %collective-permute-start.12) | collective-permute-done | bytes 16416 | tf_op jit(solution)/shard_map/ppermute | solution.py:781
  48.2 3.4 %collective-permute-done.13.refs_3_ = bf16[1,4,16,128]{3,2,1,0:T(8,128)(2,1)S(1)} collective-permute-done((bf16[1,4,16,128]{3,2,1,0:T(8,128)(2,1)S(1)}, bf16[1,4,16,128]{3,2,1,0:T(8,128)(2,1)S(1)}, u32[]{:S(2)}, u32[]{:S(2)}) %collective-permute-start.13) | collective-permute-done | bytes 16416 | tf_op jit(solution)/shard_map/ppermute | solution.py:781
  51.6 4.4 %third_layer_and_back.1 = (bf16[8,128,128]{2,1,0:T(8,128)(2,1)S(1)}, bf16[8,128,128]{2,1,0:T(8,128)(2,1)S(1)}, f32[8,128,128]{2,1,0:T(8,128)S(1)}, bf16[2,6,64,1...) custom-call(s32[13]{0:T(128)S(1)} %get-tuple-element.121.sc, ...), custom_call_target="tpu_custom_call" | custom-call | flops 603979776 | bytes 3014708 | tf_op jit(solution)/shard_map/third_layer_and_back/pallas_call | solution.py:766
  55.9 2.2 %collective-permute-start.15 = (bf16[2,6,64,128]{3,2,1,0:T(8,128)(2,1)S(1)}, bf16[2,6,64,128]{3,2,1,0:T(8,128)(2,1)S(1)}, u32[]{:S(2)}, u32[]{:S(2)}) collective-permute-start(bf16[2,6,64,128]{3,2,1,0:T(8,128)(2,1)S(1)} %get-tuple-element.156), channel_id=1, source_target_pairs={{0,8},{1,9},{2,10},{3,11},{4,12},{5,13},{6,14},{7,15},{8,0},{9,1},... | collective-permute-start | bytes 589832 | tf_op jit(solution)/shard_map/ppermute | solution.py:781
  61.8 2.1 %third_terms.1 = bf16[1152,128]{1,0:T(8,128)(2,1)S(1)} custom-call(s32[13]{0:T(128)S(1)} %get-tuple-element.121.sc, bf16[8,128,128]{2,1,0:T(8,128)(2,1)S(1)} %get-tuple-element.136.tile.second, bf16[8,128,128]{2,1,0:T(8,128)(2,1)S(1)} %get-tuple-element.153.delta.delta_third, bf16[2,6,64,128]{3,2,1,0:T(8,128)(2,1)S(1)} %collective-permute-done.10.refs_0_, ...), custom_call_target="tpu_custom_call" | custom-call | flops 301989888 | bytes 1081396 | tf_op jit(solution)/shard_map/third_terms/pallas_call | solution.py:766
  64.5 5.4 %collective-permute-done.18.refs_3_.refs_8_ = bf16[1,4,16,128]{3,2,1,0:T(8,128)(2,1)S(1)} collective-permute-done((bf16[1,4,16,128]{3,2,1,0:T(8,128)(2,1)S(1)}, bf16[1,4,16,128]{3,2,1,0:T(8,128)(2,1)S(1)}, u32[]{:S(2)}, u32[]{:S(2)}) %collective-permute-start.18) | collective-permute-done | bytes 16416 | tf_op jit(solution)/shard_map/ppermute | solution.py:781
  69.9 2.3 %second_back.1 = (bf16[8,128,128]{2,1,0:T(8,128)(2,1)S(1)}, f32[8,64,128]{2,1,0:T(8,128)S(1)}, bf16[2,6,64,128]{3,2,1,0:T(8,128)(2,1)S(1)}, bf16[3,16,128]{2,1,0...) custom-call(s32[13]{0:T(128)S(1)} %get-tuple-element.121.sc, ...), custom_call_target="tpu_custom_call" | custom-call | flops 150994944 | bytes 2113588 | tf_op jit(solution)/shard_map/second_back/pallas_call | solution.py:766
  76.5 2.5 %collective-permute-start.22 = (bf16[3,16,128]{2,1,0:T(8,128)(2,1)S(1)}, bf16[3,16,128]{2,1,0:T(8,128)(2,1)S(1)}, u32[]{:S(2)}, u32[]{:S(2)}) collective-permute-start(bf16[3,16,128]{2,1,0:T(8,128)(2,1)S(1)} %get-tuple-element.179), channel_id=1, source_target_pairs={{0,15},{1,2},{2,1},{3,4},{4,3},{5,6},{6,5},{7,8},{8,7},{9,10},{10,... | collective-permute-start | bytes 36872 | tf_op jit(solution)/shard_map/ppermute | solution.py:781
  79.0 5.5 %joined_layer_and_terms.1 = (bf16[64,16,128]{2,1,0:T(8,128)(2,1)}, bf16[1536,128]{1,0:T(8,128)(2,1)S(1)}) custom-call(s32[13]{0:T(128)S(1)} %get-tuple-element.121.sc, bf16[8,128,128]{2,1,0:T(8,128)(2,1)S(1)} %get-tuple-element.150.coarse, bf16[16,64,128]{2,1,0:T(8,128)(2,1)S(1)} %get-tuple-element.151.fine, ...), custom_call_target="tpu_custom_call" | custom-call | flops 905969664 | bytes 3506228 | tf_op jit(solution)/shard_map/joined_layer_and_terms/pallas_call | solution.py:766
  84.6 2.7 %first_back.1 = (bf16[16,64,128]{2,1,0:T(8,128)(2,1)S(1)}, f32[16,64,128]{2,1,0:T(8,128)S(1)}, bf16[2,4,64,128]{3,2,1,0:T(8,128)(2,1)S(1)}, bf16[2,16,128]{2,1,0...) custom-call(s32[13]{0:T(128)S(1)} %get-tuple-element.121.sc, ...), custom_call_target="tpu_custom_call" | custom-call | flops 150994944 | bytes 2564148 | tf_op jit(solution)/shard_map/first_back/pallas_call | solution.py:766
  96.0 1.9 %collective-permute-done.27.refs_2_ = bf16[384,128]{1,0:T(8,128)(2,1)S(1)} collective-permute-done((bf16[384,128]{1,0:T(8,128)(2,1)S(1)}, bf16[384,128]{1,0:T(8,128)(2,1)S(1)}, u32[]{:S(2)}, u32[]{:S(2)}) %collective-permute-start.27) | collective-permute-done | bytes 98336 | tf_op jit(solution)/shard_map/ppermute | solution.py:794
  99.7 3.6 %collective-permute-start.32 = (bf16[2,16,128]{2,1,0:T(8,128)(2,1)S(1)}, bf16[2,16,128]{2,1,0:T(8,128)(2,1)S(1)}, u32[]{:S(2)}, u32[]{:S(2)}) collective-permute-start(bf16[2,16,128]{2,1,0:T(8,128)(2,1)S(1)} %get-tuple-element.196), channel_id=1, source_target_pairs={{0,15},{1,2},{2,1},{3,4},{4,3},{5,6},{6,5},{7,8},{8,7},{9,10},{10,... | collective-permute-start | bytes 24584 | tf_op jit(solution)/shard_map/ppermute | solution.py:781
  104.9 2.4 %collective-permute-done.33.refs_3_ = bf16[1,1,16,128]{3,2,1,0:T(8,128)(2,1)S(1)} collective-permute-done((bf16[1,1,16,128]{3,2,1,0:T(8,128)(2,1)S(1)}, bf16[1,1,16,128]{3,2,1,0:T(8,128)(2,1)S(1)}, u32[]{:S(2)}, u32[]{:S(2)}) %collective-permute-start.33) | collective-permute-done | bytes 4128 | tf_op jit(solution)/shard_map/ppermute | solution.py:781
  109.6 1.9 %last_fold.1 = f32[64,16,128]{2,1,0:T(8,128)} custom-call(s32[13]{0:T(128)S(1)} %get-tuple-element.121.sc, f32[16,64,128]{2,1,0:T(8,128)S(1)} %get-tuple-element.200.inner, bf16[2,4,64,128]{3,2,1,0:T(8,128)(2,1)S(1)} %collective-permute-done.30.refs_0_, bf16[2,16,128]{2,1,0:T(8,128)(2,1)S(1)} %collective-permute-done.31.refs_1_, ...), custom_call_target="tpu_custom_call" | custom-call | bytes 1204276 | tf_op jit(solution)/shard_map/last_fold/pallas_call | solution.py:766
  111.5 5.6 %collective-permute-done.35.refs_1_ = bf16[384,128]{1,0:T(8,128)(2,1)S(1)} collective-permute-done((bf16[384,128]{1,0:T(8,128)(2,1)S(1)}, bf16[384,128]{1,0:T(8,128)(2,1)S(1)}, u32[]{:S(2)}, u32[]{:S(2)}) %collective-permute-start.35) | collective-permute-done | bytes 98336 | tf_op jit(solution)/shard_map/ppermute | solution.py:790
  120.7 2.6 %collective-permute-done.38.refs_3_ = bf16[384,128]{1,0:T(8,128)(2,1)S(1)} collective-permute-done((bf16[384,128]{1,0:T(8,128)(2,1)S(1)}, bf16[384,128]{1,0:T(8,128)(2,1)S(1)}, u32[]{:S(2)}, u32[]{:S(2)}) %collective-permute-start.38) | collective-permute-done | bytes 98336 | tf_op jit(solution)/shard_map/ppermute | solution.py:801
  126.1 2.0 %unpack_sums.1 = (f32[9,64,64]{2,1,0:T(8,128)}, f32[9,64,128]{2,1,0:T(8,128)}, f32[9,128,128]{2,1,0:T(8,128)}, f32[9,64,192]{2,1,0:T(8,128)}, f32[1,64]{1,0:T(1,...) custom-call(s32[13]{0:T(128)S(1)} %get-tuple-element.121.sc, bf16[384,128]{1,0:T(8,128)(2,1)S(1)} %sum_3.1.refs_0_, ...), custom_call_target="tpu_custom_call" | custom-call | bytes 2262580 | tf_op jit(solution)/shard_map/unpack_sums/pallas_call | solution.py:766
  (102 shorter events, 48.9 us)
Async XLA Ops:
  3.3 15.5 %collective-permute-start = (bf16[2,17,16,128]{3,2,1,0:T(8,128)(2,1)S(1)}, bf16[2,17,16,128]{3,2,1,0:T(8,128)(2,1)S(1)}, u32[]{:S(2)}, u32[]{:S(2)}) collective-permute-start(bf16[2,17,16,128]{3,2,1,0:T(8,128)(2,1)S(1)} %get-tuple-element.114), channel_id=1, source_target_pairs={{0,8},{1,9},{2,10},{3,11},{4,12},{5,13},{6,14},{7,15},{8,0},{9,1},... | collective-permute-start | bytes 417800 | tf_op jit(solution)/shard_map/ppermute | solution.py:781
  7.4 11.4 %collective-permute-start.1 = (bf16[2,16,128]{2,1,0:T(8,128)(2,1)S(1)}, bf16[2,16,128]{2,1,0:T(8,128)(2,1)S(1)}, u32[]{:S(2)}, u32[]{:S(2)}) collective-permute-start(bf16[2,16,128]{2,1,0:T(8,128)(2,1)S(1)} %get-tuple-element.115), channel_id=1, source_target_pairs={{0,1},{1,0},{2,3},{3,2},{4,5},{5,4},{6,7},{7,6},{8,9},{9,8},{10,11... | collective-permute-start | bytes 24584 | tf_op jit(solution)/shard_map/ppermute | solution.py:781
  7.4 11.4 %collective-permute-start.2 = (bf16[2,16,128]{2,1,0:T(8,128)(2,1)S(1)}, bf16[2,16,128]{2,1,0:T(8,128)(2,1)S(1)}, u32[]{:S(2)}, u32[]{:S(2)}) collective-permute-start(bf16[2,16,128]{2,1,0:T(8,128)(2,1)S(1)} %get-tuple-element.116), channel_id=1, source_target_pairs={{0,15},{1,2},{2,1},{3,4},{4,3},{5,6},{6,5},{7,8},{8,7},{9,10},{10,... | collective-permute-start | bytes 24584 | tf_op jit(solution)/shard_map/ppermute | solution.py:781
  9.8 8.9 %collective-permute-start.3 = (bf16[1,1,16,128]{3,2,1,0:T(8,128)(2,1)S(1)}, bf16[1,1,16,128]{3,2,1,0:T(8,128)(2,1)S(1)}, u32[]{:S(2)}, u32[]{:S(2)}) collective-permute-start(bf16[1,1,16,128]{3,2,1,0:T(8,128)(2,1)S(1)} %get-tuple-element.117), channel_id=1, source_target_pairs={{0,9},{1,8},{2,11},{3,10},{4,13},{5,12},{6,15},{7,14},{8,1},{9,0},... | collective-permute-start | bytes 12296 | tf_op jit(solution)/shard_map/ppermute | solution.py:781
  9.8 8.9 %collective-permute-start.4 = (bf16[1,1,16,128]{3,2,1,0:T(8,128)(2,1)S(1)}, bf16[1,1,16,128]{3,2,1,0:T(8,128)(2,1)S(1)}, u32[]{:S(2)}, u32[]{:S(2)}) collective-permute-start(bf16[1,1,16,128]{3,2,1,0:T(8,128)(2,1)S(1)} %get-tuple-element.118), channel_id=1, source_target_pairs={{0,7},{1,10},{2,9},{3,12},{4,11},{5,14},{6,13},{7,0},{8,15},{9,2},... | collective-permute-start | bytes 12296 | tf_op jit(solution)/shard_map/ppermute | solution.py:781
  22.6 14.0 %collective-permute-start.5 = (bf16[2,6,64,128]{3,2,1,0:T(8,128)(2,1)S(1)}, bf16[2,6,64,128]{3,2,1,0:T(8,128)(2,1)S(1)}, u32[]{:S(2)}, u32[]{:S(2)}) collective-permute-start(bf16[2,6,64,128]{3,2,1,0:T(8,128)(2,1)S(1)} %get-tuple-element.123), channel_id=1, source_target_pairs={{0,8},{1,9},{2,10},{3,11},{4,12},{5,13},{6,14},{7,15},{8,0},{9,1},... | collective-permute-start | bytes 589832 | tf_op jit(solution)/shard_map/ppermute | solution.py:781
  25.2 11.3 %collective-permute-start.8 = (bf16[1,2,16,128]{3,2,1,0:T(8,128)(2,1)S(1)}, bf16[1,2,16,128]{3,2,1,0:T(8,128)(2,1)S(1)}, u32[]{:S(2)}, u32[]{:S(2)}) collective-permute-start(bf16[1,2,16,128]{3,2,1,0:T(8,128)(2,1)S(1)} %get-tuple-element.126), channel_id=1, source_target_pairs={{0,9},{1,8},{2,11},{3,10},{4,13},{5,12},{6,15},{7,14},{8,1},{9,0},... | collective-permute-start | bytes 24584 | tf_op jit(solution)/shard_map/ppermute | solution.py:781
  26.9 9.7 %collective-permute-start.9 = (bf16[1,2,16,128]{3,2,1,0:T(8,128)(2,1)S(1)}, bf16[1,2,16,128]{3,2,1,0:T(8,128)(2,1)S(1)}, u32[]{:S(2)}, u32[]{:S(2)}) collective-permute-start(bf16[1,2,16,128]{3,2,1,0:T(8,128)(2,1)S(1)} %get-tuple-element.127), channel_id=1, source_target_pairs={{0,7},{1,10},{2,9},{3,12},{4,11},{5,14},{6,13},{7,0},{8,15},{9,2},... | collective-permute-start | bytes 24584 | tf_op jit(solution)/shard_map/ppermute | solution.py:781
  38.5 13.0 %collective-permute-start.10 = (bf16[2,6,64,128]{3,2,1,0:T(8,128)(2,1)S(1)}, bf16[2,6,64,128]{3,2,1,0:T(8,128)(2,1)S(1)}, u32[]{:S(2)}, u32[]{:S(2)}) collective-permute-start(bf16[2,6,64,128]{3,2,1,0:T(8,128)(2,1)S(1)} %get-tuple-element.137), channel_id=1, source_target_pairs={{0,8},{1,9},{2,10},{3,11},{4,12},{5,13},{6,14},{7,15},{8,0},{9,1},... | collective-permute-start | bytes 589832 | tf_op jit(solution)/shard_map/ppermute | solution.py:781
  39.5 8.7 %collective-permute-start.12 = (bf16[4,16,128]{2,1,0:T(8,128)(2,1)S(1)}, bf16[4,16,128]{2,1,0:T(8,128)(2,1)S(1)}, u32[]{:S(2)}, u32[]{:S(2)}) collective-permute-start(bf16[4,16,128]{2,1,0:T(8,128)(2,1)S(1)} %get-tuple-element.139), channel_id=1, source_target_pairs={{0,15},{1,2},{2,1},{3,4},{4,3},{5,6},{6,5},{7,8},{8,7},{9,10},{10,... | collective-permute-start | bytes 49160 | tf_op jit(solution)/shard_map/ppermute | solution.py:781
  42.7 8.8 %collective-permute-start.13 = (bf16[1,4,16,128]{3,2,1,0:T(8,128)(2,1)S(1)}, bf16[1,4,16,128]{3,2,1,0:T(8,128)(2,1)S(1)}, u32[]{:S(2)}, u32[]{:S(2)}) collective-permute-start(bf16[1,4,16,128]{3,2,1,0:T(8,128)(2,1)S(1)} %get-tuple-element.140), channel_id=1, source_target_pairs={{0,9},{1,8},{2,11},{3,10},{4,13},{5,12},{6,15},{7,14},{8,1},{9,0},... | collective-permute-start | bytes 49160 | tf_op jit(solution)/shard_map/ppermute | solution.py:781
  42.7 8.8 %collective-permute-start.14 = (bf16[1,4,16,128]{3,2,1,0:T(8,128)(2,1)S(1)}, bf16[1,4,16,128]{3,2,1,0:T(8,128)(2,1)S(1)}, u32[]{:S(2)}, u32[]{:S(2)}) collective-permute-start(bf16[1,4,16,128]{3,2,1,0:T(8,128)(2,1)S(1)} %get-tuple-element.141), channel_id=1, source_target_pairs={{0,7},{1,10},{2,9},{3,12},{4,11},{5,14},{6,13},{7,0},{8,15},{9,2},... | collective-permute-start | bytes 49160 | tf_op jit(solution)/shard_map/ppermute | solution.py:781
  55.9 13.9 %collective-permute-start.15 = (bf16[2,6,64,128]{3,2,1,0:T(8,128)(2,1)S(1)}, bf16[2,6,64,128]{3,2,1,0:T(8,128)(2,1)S(1)}, u32[]{:S(2)}, u32[]{:S(2)}) collective-permute-start(bf16[2,6,64,128]{3,2,1,0:T(8,128)(2,1)S(1)} %get-tuple-element.156), channel_id=1, source_target_pairs={{0,8},{1,9},{2,10},{3,11},{4,12},{5,13},{6,14},{7,15},{8,0},{9,1},... | collective-permute-start | bytes 589832 | tf_op jit(solution)/shard_map/ppermute | solution.py:781
  59.5 10.3 %collective-permute-start.18 = (bf16[1,4,16,128]{3,2,1,0:T(8,128)(2,1)S(1)}, bf16[1,4,16,128]{3,2,1,0:T(8,128)(2,1)S(1)}, u32[]{:S(2)}, u32[]{:S(2)}) collective-permute-start(bf16[1,4,16,128]{3,2,1,0:T(8,128)(2,1)S(1)} %get-tuple-element.159), channel_id=1, source_target_pairs={{0,9},{1,8},{2,11},{3,10},{4,13},{5,12},{6,15},{7,14},{8,1},{9,0},... | collective-permute-start | bytes 49160 | tf_op jit(solution)/shard_map/ppermute | solution.py:781
  60.5 9.4 %collective-permute-start.19 = (bf16[1,4,16,128]{3,2,1,0:T(8,128)(2,1)S(1)}, bf16[1,4,16,128]{3,2,1,0:T(8,128)(2,1)S(1)}, u32[]{:S(2)}, u32[]{:S(2)}) collective-permute-start(bf16[1,4,16,128]{3,2,1,0:T(8,128)(2,1)S(1)} %get-tuple-element.160), channel_id=1, source_target_pairs={{0,7},{1,10},{2,9},{3,12},{4,11},{5,14},{6,13},{7,0},{8,15},{9,2},... | collective-permute-start | bytes 49160 | tf_op jit(solution)/shard_map/ppermute | solution.py:781
  72.2 12.4 %collective-permute-start.20 = (bf16[2,6,64,128]{3,2,1,0:T(8,128)(2,1)S(1)}, bf16[2,6,64,128]{3,2,1,0:T(8,128)(2,1)S(1)}, u32[]{:S(2)}, u32[]{:S(2)}) collective-permute-start(bf16[2,6,64,128]{3,2,1,0:T(8,128)(2,1)S(1)} %get-tuple-element.175), channel_id=1, source_target_pairs={{0,8},{1,9},{2,10},{3,11},{4,12},{5,13},{6,14},{7,15},{8,0},{9,1},... | collective-permute-start | bytes 589832 | tf_op jit(solution)/shard_map/ppermute | solution.py:781
  73.3 11.3 %collective-permute-start.23 = (bf16[1,2,16,128]{3,2,1,0:T(8,128)(2,1)S(1)}, bf16[1,2,16,128]{3,2,1,0:T(8,128)(2,1)S(1)}, u32[]{:S(2)}, u32[]{:S(2)}) collective-permute-start(bf16[1,2,16,128]{3,2,1,0:T(8,128)(2,1)S(1)} %get-tuple-element.180), channel_id=1, source_target_pairs={{0,9},{1,8},{2,11},{3,10},{4,13},{5,12},{6,15},{7,14},{8,1},{9,0},... | collective-permute-start | bytes 24584 | tf_op jit(solution)/shard_map/ppermute | solution.py:781
  74.6 9.9 %collective-permute-start.24 = (bf16[1,2,16,128]{3,2,1,0:T(8,128)(2,1)S(1)}, bf16[1,2,16,128]{3,2,1,0:T(8,128)(2,1)S(1)}, u32[]{:S(2)}, u32[]{:S(2)}) collective-permute-start(bf16[1,2,16,128]{3,2,1,0:T(8,128)(2,1)S(1)} %get-tuple-element.181), channel_id=1, source_target_pairs={{0,7},{1,10},{2,9},{3,12},{4,11},{5,14},{6,13},{7,0},{8,15},{9,2},... | collective-permute-start | bytes 24584 | tf_op jit(solution)/shard_map/ppermute | solution.py:781
  75.4 9.1 %collective-permute-start.21 = (bf16[3,16,128]{2,1,0:T(8,128)(2,1)S(1)}, bf16[3,16,128]{2,1,0:T(8,128)(2,1)S(1)}, u32[]{:S(2)}, u32[]{:S(2)}) collective-permute-start(bf16[3,16,128]{2,1,0:T(8,128)(2,1)S(1)} %get-tuple-element.178), channel_id=1, source_target_pairs={{0,1},{1,0},{2,3},{3,2},{4,5},{5,4},{6,7},{7,6},{8,9},{9,8},{10,11... | collective-permute-start | bytes 36872 | tf_op jit(solution)/shard_map/ppermute | solution.py:781
  76.5 8.0 %collective-permute-start.22 = (bf16[3,16,128]{2,1,0:T(8,128)(2,1)S(1)}, bf16[3,16,128]{2,1,0:T(8,128)(2,1)S(1)}, u32[]{:S(2)}, u32[]{:S(2)}) collective-permute-start(bf16[3,16,128]{2,1,0:T(8,128)(2,1)S(1)} %get-tuple-element.179), channel_id=1, source_target_pairs={{0,15},{1,2},{2,1},{3,4},{4,3},{5,6},{6,5},{7,8},{8,7},{9,10},{10,... | collective-permute-start | bytes 36872 | tf_op jit(solution)/shard_map/ppermute | solution.py:781
  94.6 14.2 %collective-permute-start.30 = (bf16[2,4,64,128]{3,2,1,0:T(8,128)(2,1)S(1)}, bf16[2,4,64,128]{3,2,1,0:T(8,128)(2,1)S(1)}, u32[]{:S(2)}, u32[]{:S(2)}) collective-permute-start(bf16[2,4,64,128]{3,2,1,0:T(8,128)(2,1)S(1)} %get-tuple-element.194), channel_id=1, source_target_pairs={{0,8},{1,9},{2,10},{3,11},{4,12},{5,13},{6,14},{7,15},{8,0},{9,1},... | collective-permute-start | bytes 393224 | tf_op jit(solution)/shard_map/ppermute | solution.py:781
  99.7 9.1 %collective-permute-start.31 = (bf16[2,16,128]{2,1,0:T(8,128)(2,1)S(1)}, bf16[2,16,128]{2,1,0:T(8,128)(2,1)S(1)}, u32[]{:S(2)}, u32[]{:S(2)}) collective-permute-start(bf16[2,16,128]{2,1,0:T(8,128)(2,1)S(1)} %get-tuple-element.195), channel_id=1, source_target_pairs={{0,1},{1,0},{2,3},{3,2},{4,5},{5,4},{6,7},{7,6},{8,9},{9,8},{10,11... | collective-permute-start | bytes 24584 | tf_op jit(solution)/shard_map/ppermute | solution.py:781
  99.7 9.1 %collective-permute-start.32 = (bf16[2,16,128]{2,1,0:T(8,128)(2,1)S(1)}, bf16[2,16,128]{2,1,0:T(8,128)(2,1)S(1)}, u32[]{:S(2)}, u32[]{:S(2)}) collective-permute-start(bf16[2,16,128]{2,1,0:T(8,128)(2,1)S(1)} %get-tuple-element.196), channel_id=1, source_target_pairs={{0,15},{1,2},{2,1},{3,4},{4,3},{5,6},{6,5},{7,8},{8,7},{9,10},{10,... | collective-permute-start | bytes 24584 | tf_op jit(solution)/shard_map/ppermute | solution.py:781
  108.8 8.3 %collective-permute-start.35 = (bf16[384,128]{1,0:T(8,128)(2,1)S(1)}, bf16[384,128]{1,0:T(8,128)(2,1)S(1)}, u32[]{:S(2)}, u32[]{:S(2)}) collective-permute-start(bf16[384,128]{1,0:T(8,128)(2,1)S(1)} %sum_2.1.refs_0_), channel_id=1, source_target_pairs={{0,8},{1,9},{2,10},{3,11},{4,12},{5,13},{6,14},{7,15},{8,0},{9,1},... | collective-permute-start | bytes 294920 | tf_op jit(solution)/shard_map/ppermute | solution.py:790
  (29 other events, 124.5 us)
where the time goes:
time: 128 us
  starting transfers between devices  46.7 us (36%)
  Pallas kernels  38 us (30%)
  waiting for transfers between devices  34.4 us (27%)
  local copies, waits for them, and re-layouts  8.07 us (6%)
    ppermute x30, starting transfers between devices, shifted(): return lax.ppermute(array, 'tile', pairs)  38.4 us
    pallas_call x18, Pallas kernels, call(): pl.pallas_call(body, out_shape=[jax.ShapeDtypeStruct(shape, kind) for sha...  38 us
    ppermute x30, waiting for transfers between devices, shifted(): return lax.ppermute(array, 'tile', pairs)  16.7 us
    ppermute x9, waiting for transfers between devices, other_tile(): return lax.ppermute(array, 'tile', pairs)  10.6 us
    unnamed x20, local copies, waits for them, and re-layouts  7.31 us
    ppermute x2, waiting for transfers between devices, other_both(): return lax.ppermute(array, ('ens', 'tile'), pairs)  4.23 us
    ppermute x9, starting transfers between devices, other_tile(): return lax.ppermute(array, 'tile', pairs)  3.92 us
    ppermute x2, waiting for transfers between devices, other_member(): return lax.ppermute(array, 'ens', [(0, 1), (1, 0)])  2.88 us
  transfers between devices with their start and end apart: 43, of which 17 were waited for; matrix products, arithmetic and copies ran while one was open for 0% of the time, Pallas kernels for 14%

commit v1 on v0

--- a/solution.py
+++ b/solution.py
@@ -293,14 +293,6 @@
     return jnp.where(jnp.bitwise_and(row, LANES - 1) // 2 == col, weight, 0.0).astype(BF16)
 
 
-def side_pool_matrix():
-    row = lax.broadcasted_iota(jnp.int32, (2 * LANES, LANES), 0)
-    col = lax.broadcasted_iota(jnp.int32, (2 * LANES, LANES), 1)
-    row = jnp.bitwise_and(row, LANES - 1)
-    target = jnp.where(row >= 124, 126 + (row - 124) // 2, jnp.where(row < 4, 64 + row // 2, -1))
-    return jnp.where(target == col, 1.0, 0.0).astype(BF16)
-
-
 def spread_matrix():
     row = lax.broadcasted_iota(jnp.int32, (LANES, LANES), 0)
     col = lax.broadcasted_iota(jnp.int32, (LANES, LANES), 1)
@@ -323,33 +315,37 @@
         delta[8 + r] = rows(r)
 
 
+def tap_products(delta, kernel, spacing, r):
+    sections = []
+    for row in (r, r + 1):
+        sections.append(
+            jnp.concatenate([delta[8 + row - DMAX - (a - 1) * spacing] for a in range(3)], axis=0)
+        )
+    return matmul(kernel[...], jnp.concatenate(sections, axis=1))
+
+
+def move_taps(left, middle, right, spacing, width):
+    lane = lane_of(middle.shape)
+    to_left, to_right = turn(left, -spacing), turn(right, spacing)
+    if width == 64:
+        own = middle + to_left + to_right
+        return own, own
+    keep_right = lane >= spacing
+    keep_left = lane < LANES - spacing
+    own = middle + jnp.where(keep_right, to_right, 0.0) + jnp.where(keep_left, to_left, 0.0)
+    sides = jnp.where(keep_right, 0.0, to_right) + jnp.where(keep_left, 0.0, to_left)
+    return own, sides
+
+
 def spread_taps(delta, kernel, spacing, width):
     count = delta.shape[0] - 16
     channels = kernel.shape[0] // 3
-    lane = lane_of((channels, LANES))
     for r in range(0, count + 2 * DMAX, 2):
-        sections = []
-        for row in (r, r + 1):
-            sections.append(
-                jnp.concatenate(
-                    [delta[8 + row - DMAX - (a - 1) * spacing] for a in range(3)], axis=0
-                )
-            )
-        both = matmul(kernel[...], jnp.concatenate(sections, axis=1))
+        both = tap_products(delta, kernel, spacing, r)
         for k in range(2):
             part = both[:, k * LANES : (k + 1) * LANES]
-            to_left = turn(part[:channels], -spacing)
-            own = part[channels : 2 * channels]
-            to_right = turn(part[2 * channels :], spacing)
-            if width == 64:
-                own = own + to_left + to_right
-                yield r + k, own, own
-            else:
-                keep_right = lane >= spacing
-                keep_left = lane < LANES - spacing
-                own = own + jnp.where(keep_right, to_right, 0.0) + jnp.where(keep_left, to_left, 0.0)
-                sides = jnp.where(keep_right, 0.0, to_right) + jnp.where(keep_left, 0.0, to_left)
-                yield r + k, own, sides
+            pieces = [part[e * channels : (e + 1) * channels] for e in range(3)]
+            yield (r + k,) + move_taps(*pieces, spacing, width)
 
 
 def rim_messages(own, sides, sends, places, width, margin, sc):
@@ -427,29 +423,36 @@
 AFTER_SECOND = (4, 2, 2)
 
 
-def weights_kernel(swapped, *refs):
-    kernels, arrived = refs[20:24], refs[24]
-    copies = [pltpu.make_async_copy(refs[i], kernels[i], arrived.at[i]) for i in range(4)]
-    for copy in copies:
-        copy.start()
-    for i, (kernel, offset) in enumerate(zip(kernels, refs[4:8])):
-        forward, backward, shift = refs[8 + i], refs[12 + i], refs[16 + i]
-        copies[i].wait()
-        outs, channels = kernel.shape[1:]
-        if swapped[i]:
-            outs, channels = channels, outs
+def weights_kernel(jobs, swapped, *refs):
+    layers = sorted({layer for _, layer in jobs})
+    kernels = dict(zip(layers, refs))
+    shifts = [layer for form, layer in jobs if form == 2]
+    offsets = dict(zip(shifts, refs[len(layers) :]))
+    outs = dict(zip(jobs, refs[len(layers) + len(shifts) :]))
+    for layer in layers:
+        kernel = kernels[layer]
+        count, channels = kernel.shape[1:]
+        if swapped[layer]:
+            count, channels = channels, count
         for tap in range(9):
             a, e = tap // 3, tap % 3
-            own = kernel[tap]
-            across = jnp.transpose(own.astype(F32)).astype(BF16)
-            if swapped[i]:
-                own, across = across, own
-            forward[:, tap * channels : (tap + 1) * channels] = own
-            backward[e * channels : (e + 1) * channels, a * outs : (a + 1) * outs] = across
-        row = lax.broadcasted_iota(jnp.int32, (outs, outs), 0)
-        col = lax.broadcasted_iota(jnp.int32, (outs, outs), 1)
-        column = jnp.sum(jnp.where(row == col, offset[...], 0.0), axis=1, keepdims=True)
-        shift[...] = jnp.broadcast_to(column, shift.shape)
+            for form in range(2):
+                if (form, layer) not in outs:
+                    continue
+                part = kernel[tap]
+                if (form == 1) != swapped[layer]:
+                    part = jnp.transpose(part.astype(F32)).astype(BF16)
+                if form == 0:
+                    outs[0, layer][:, tap * channels : (tap + 1) * channels] = part
+                else:
+                    rows = slice(e * channels, (e + 1) * channels)
+                    outs[1, layer][rows, a * count : (a + 1) * count] = part
+        if (2, layer) in outs:
+            row = lax.broadcasted_iota(jnp.int32, (count, count), 0)
+            col = lax.broadcasted_iota(jnp.int32, (count, count), 1)
+            column = jnp.where(row == col, offsets[layer][...], 0.0)
+            column = jnp.sum(column, axis=1, keepdims=True)
+            outs[2, layer][...] = jnp.broadcast_to(column, outs[2, layer].shape)
 
 
 def fields_kernel(sc, fields, tile, *sends):
@@ -498,11 +501,10 @@
     shift = column_of(offset)
     for i in range(0, tile.shape[0], 2):
         pre = matmul(kernel[...], tap_pair(taps, i, spacing)) + shift
-        both = beside(pre[:, :LANES], pre[:, LANES:])
-        act = gelu(both).astype(BF16)
+        act = gelu(pre).astype(BF16)
         for k in range(2):
-            act_out[i + k] = turn(act, 64 * k)
-        pre_out[i // 2] = both
+            act_out[i + k] = act[:, k * LANES : (k + 1) * LANES]
+            pre_out[i + k] = pre[:, k * LANES : (k + 1) * LANES]
     edge_messages(lambda r: act_out[r], act_out, sends, START, 64, DMAX, sc)
     pass_on(extras, sends, AFTER_SECOND)
 
@@ -514,12 +516,8 @@
             out[r] = gelu_slope(values[r])
 
 
-def beside(first, second):
-    return jnp.where(lane_of(first.shape) < 64, first, turn(second, 64))
-
-
 def masked(values, width):
-    return jnp.where(lane_of(values.shape) < width, values, jnp.zeros_like(values))
+    return jnp.where(lane_of(values.shape) < width, values, 0.0).astype(BF16)
 
 
 def back_part(sc, delta, kernel, spacing, width, inner_out, sends, own_all, sides_all):
@@ -543,12 +541,12 @@
     shift = column_of(offset)
     for i in range(0, tile.shape[0], 2):
         pre = matmul(kernel[...], tap_pair(taps, i, spacing)) + shift
-        both = beside(pre[:, :LANES], pre[:, LANES:])
-        act = gelu(both).astype(BF16)
-        change = (beside(coarse_sum[i], coarse_sum[i + 1]) * gelu_slope(both)).astype(BF16)
+        act, slope = gelu(pre), gelu_slope(pre)
         for k in range(2):
-            act_out[i + k] = turn(act, 64 * k)
-            delta_out[i + k] = masked(turn(change, 64 * k), 64)
+            act_out[i + k] = act[:, k * LANES : (k + 1) * LANES].astype(BF16)
+            delta_out[i + k] = masked(
+                coarse_sum[i + k] * slope[:, k * LANES : (k + 1) * LANES], 64
+            )
     fill_delta(delta, lambda r: delta_out[r])
     back_part(sc, delta, back, spacing, 64, inner_out, sends, own_all, own_all)
     edge_messages(lambda r: act_out[r], act_out, sends, AFTER_SECOND, 64, 2, sc)
@@ -559,10 +557,8 @@
     delta_out, inner_out = refs[12:14]
     sends, (total, delta, own_all) = refs[14:19], refs[19:]
     fold(total, inner, received, START, 64, DMAX, sc)
-    for r in range(0, inner.shape[0], 2):
-        change = (beside(total[r], total[r + 1]) * slope[r // 2]).astype(BF16)
-        for k in range(2):
-            delta_out[r + k] = masked(turn(change, 64 * k), 64)
+    for r in range(inner.shape[0]):
+        delta_out[r] = masked(total[r] * slope[r], 64)
     fill_delta(delta, lambda r: delta_out[r])
     back_part(sc, delta, back, sc[7], 64, inner_out, sends, own_all, own_all)
     pass_on(extras, sends, AFTER_POOLED)
@@ -592,25 +588,46 @@
     out[...] = jnp.swapaxes(total[...], 0, 1)
 
 
-def upstream_kernel(sc, cotangent, back, *refs):
+def moved_pool_matrix(spacing):
+    row = lax.broadcasted_iota(jnp.int32, (2 * LANES, LANES), 0)
+    col = lax.broadcasted_iota(jnp.int32, (2 * LANES, LANES), 1)
+    parts = []
+    for e in range(3):
+        target = jnp.right_shift(jnp.bitwise_and(row, LANES - 1) + (e - 1) * spacing, 1)
+        hit = jnp.bitwise_and(target, LANES - 1) == col
+        parts.append(jnp.where(hit, 1.0, 0.0).astype(BF16))
+    return jnp.concatenate(parts, axis=0)
+
+
+def upstream_kernel(sc, cotangent, closing, *refs):
     upstream, coarse_out, skip_out = refs[:3]
     coarse_sends, skip_sends = refs[3:8], refs[8:13]
-    delta, own_all, sides_all, coarse_all = refs[13:]
+    delta, own_all, sides_all, coarse_all, back, high_all, low_all = refs[13:]
+    outs, channels = closing.shape[1:]
+    for tap in range(9):
+        a, e = tap // 3, tap % 3
+        across = jnp.transpose(closing[tap].astype(F32)).astype(BF16)
+        back[e * channels : (e + 1) * channels, a * outs : (a + 1) * outs] = across
     upstream[...] = jnp.swapaxes(cotangent[...], 0, 1)
     fill_delta(delta, lambda r: upstream[r])
-    pool = jnp.concatenate([pool_matrix(1.0), side_pool_matrix()], axis=0)
-    pending = None
-    for r, own, sides in spread_taps(delta, back, sc[9], LANES):
-        own_all[r] = own[128:]
-        sides_all[r] = sides[128:]
-        if pending is None:
-            pending = (own[:128], sides[:128])
-        else:
-            high, low = halves(
-                jnp.concatenate([pending[0], own[:128], pending[1], sides[:128]], axis=1)
-            )
-            coarse_all[r // 2] = matmul(high, pool) + matmul(low, pool)
-            pending = None
+    spacing = sc[9]
+    pool = moved_pool_matrix(spacing)
+    skips = own_all.shape[1]
+    coarse = channels - skips
+    for r in range(0, own_all.shape[0], 2):
+        both = tap_products(delta, back, spacing, r)
+        parts = [both[e * channels : (e + 1) * channels] for e in range(3)]
+        high, low = halves(jnp.concatenate([part[:coarse] for part in parts], axis=1))
+        at = r // 2 * coarse
+        high_all[at : at + coarse] = high
+        low_all[at : at + coarse] = low
+        for k in range(2):
+            lanes = slice(k * LANES, (k + 1) * LANES)
+            own, sides = move_taps(*[part[coarse:, lanes] for part in parts], spacing, LANES)
+            own_all[r + k] = own
+            sides_all[r + k] = sides
+    pooled = matmul(high_all[...], pool) + matmul(low_all[...], pool)
+    coarse_all[...] = pooled.reshape(coarse_all.shape)
     for r in range(coarse_out.shape[0]):
         coarse_out[r] = coarse_all[2 + r]
     for r in range(skip_out.shape[0]):
@@ -754,10 +771,8 @@
         out[...] = jnp.sum(jnp.where(row == col, column, 0.0), axis=0, keepdims=True) * scale
 
 
-def call(body, inputs, outputs, scratch=(), flops=0, scalars=1, copied=0, name=None):
+def call(body, inputs, outputs, scratch=(), flops=0, scalars=1, name=None):
     specs = [pl.BlockSpec(memory_space=pltpu.VMEM)] * len(inputs)
-    specs[:copied] = [pl.BlockSpec(memory_space=pl.ANY)] * copied
-    arrived = [pltpu.SemaphoreType.DMA((copied,))] if copied else []
     for i in range(scalars):
         specs[i] = pl.BlockSpec(memory_space=pltpu.SMEM)
     moved = sum(math.prod(shape) * jnp.dtype(kind).itemsize for shape, kind in outputs)
@@ -768,7 +783,7 @@
         out_shape=[jax.ShapeDtypeStruct(shape, kind) for shape, kind in outputs],
         in_specs=specs,
         out_specs=[pl.BlockSpec(memory_space=space) for space in spaces],
-        scratch_shapes=[pltpu.VMEM(shape, kind) for shape, kind in scratch] + arrived,
+        scratch_shapes=[pltpu.VMEM(shape, kind) for shape, kind in scratch],
         compiler_params=pltpu.CompilerParams(vmem_limit_bytes=24 * 1024 * 1024),
         cost_estimate=pl.CostEstimate(flops=flops, bytes_accessed=moved, transcendentals=0),
         name=name,
@@ -870,27 +885,29 @@
     weights = [kernel_first, kernel_second, kernel_third, closing_filter_weights]
     offsets = [offset_first, offset_second, offset_third, closing_shift_values]
     swapped = [k.shape[1] % LANES == 0 and k.shape[2] % LANES != 0 for k in weights]
-    forms = call(
-        functools.partial(weights_kernel, swapped),
-        [jnp.swapaxes(k, 1, 2) if swap else k for k, swap in zip(weights, swapped)]
-        + [offset[None] for offset in offsets],
-        scratch=[
-            ((9, k.shape[2], k.shape[1]) if swap else k.shape, BF16)
-            for k, swap in zip(weights, swapped)
-        ],
-        copied=4,
-        outputs=        [((k.shape[1], 9 * k.shape[2]), BF16) for k in weights]
-        + [((3 * k.shape[2], 3 * k.shape[1]), BF16) for k in weights]
-        + [((k.shape[1], LANES), F32) for k in weights],
-        scalars=0,
-        name="weights",
-    )
-    forward, backward, shifts = forms[:4], forms[4:8], forms[8:]
+    def prepare(jobs, kernels, name):
+        layers = sorted({layer for _, layer in jobs})
+        inputs = [jnp.swapaxes(kernels[i], 1, 2) if swapped[i] else kernels[i] for i in layers]
+        outputs = []
+        for form, layer in jobs:
+            _, count, channels = kernels[layer].shape
+            shapes = [(count, 9 * channels), (3 * channels, 3 * count), (count, LANES)]
+            outputs.append((shapes[form], F32 if form == 2 else BF16))
+        made = call(
+            functools.partial(weights_kernel, jobs, swapped),
+            inputs + [offsets[layer][None] for form, layer in jobs if form == 2],
+            outputs,
+            scalars=0,
+            name=name,
+        )
+        return dict(zip(jobs, made))
+
+    forms = prepare([(0, 0), (0, 1), (2, 0), (2, 1)], weights, "early_weights")
 
     first_taps = ((height + 8, 3 * low, LANES), BF16)
     act_first, pre_first, pooled, sc, taps_first, *sent = call(
         first_kernel,
-        [own_sc, tile, *first_in, forward[0], shifts[0]],
+        [own_sc, tile, *first_in, forms[0, 0], forms[2, 0]],
         [fine_tile, fine_grad, ((half, low, LANES), BF16), ((13,), jnp.int32), first_taps]
         + sends(6, 3, 2),
         flops=2 * 9 * low * low * height * width,
@@ -900,13 +917,16 @@
 
     upstream, coarse_inner, skip_inner, *rims = call(
         upstream_kernel,
-        [sc, cotangent[0, 0], backward[3]],
+        [sc, cotangent[0, 0], closing_filter_weights],
         [fine_tile, ((half, high, LANES), F32), fine_grad] + sends(2, 2, 2) + sends(4, 2, 1),
         [
             ((height + 16, low, LANES), BF16),
             ((height + 8, low, LANES), F32),
             ((height + 8, low, LANES), F32),
             ((half + 4, high, LANES), F32),
+            ((3 * (low + high), 3 * low), BF16),
+            (((half + 4) * high, 6 * LANES), BF16),
+            (((half + 4) * high, 6 * LANES), BF16),
         ],
         flops=2 * 9 * low * (low + high) * height * width,
         name="cotangent_back",
@@ -916,17 +936,25 @@
     second_taps = ((half + 8, 3 * low, LANES), BF16)
     act_second, pre_second, taps_second, *sent = call(
         second_kernel,
-        [sc, pooled, *second_in, forward[1], shifts[1], *coarse_rims],
-        [((half, high, LANES), BF16), ((half // 2, high, LANES), F32), second_taps]
+        [sc, pooled, *second_in, forms[0, 1], forms[2, 1], *coarse_rims],
+        [((half, high, LANES), BF16), ((half, high, LANES), F32), second_taps]
         + sends(6, 4, 4),
         flops=2 * 9 * low * high * half * LANES,
         name="second_layer",
     )
     third_in = exchange(*sent)
+    late_third, pre_second = lax.optimization_barrier((kernel_third, pre_second))
+    forms.update(
+        prepare(
+            [(0, 2), (0, 3), (1, 0), (1, 1), (1, 2), (2, 2), (2, 3)],
+            weights[:2] + [late_third] + weights[3:],
+            "late_weights",
+        )
+    )
     slope_first, slope_second = call(
         slopes_kernel,
         [pre_first, pre_second],
-        [fine_grad, ((half // 2, high, LANES), F32)],
+        [fine_grad, ((half, high, LANES), F32)],
         scalars=0,
         name="slopes",
     )
@@ -935,7 +963,7 @@
     third_taps = ((half + 8, 3 * high, LANES), BF16)
     act_third, delta_third, inner, *sent = call(
         third_kernel,
-        [sc, act_second, *third_in, forward[2], shifts[2], coarse_inner, backward[2]],
+        [sc, act_second, *third_in, forms[0, 2], forms[2, 2], coarse_inner, forms[1, 2]],
         [((half, high, LANES), BF16)] * 2 + [((half, high, LANES), F32)] + sends(6, 4, 4),
         [
             third_taps,
@@ -959,7 +987,7 @@
 
     delta_second, inner, *sent = call(
         middle_kernel,
-        [sc, inner, *back_in, slope_second, backward[1], *skip_rims],
+        [sc, inner, *back_in, slope_second, forms[1, 1], *skip_rims],
         [((half, high, LANES), BF16), ((half, low, LANES), F32)] + sends(6, 3, 2),
         [
             ((half, high, LANES), F32),
@@ -977,8 +1005,8 @@
     state, upper_terms = call(
         joined_kernel,
         [
-            sc, act_third, act_first, taps_second, delta_third, delta_second, upstream, forward[3],
-            shifts[3], *second_in, *back_in,
+            sc, act_third, act_first, taps_second, delta_third, delta_second, upstream, forms[0, 3],
+            forms[2, 3], *second_in, *back_in,
         ],
         [((low, height, LANES), BF16), ((upper_rows, LANES), BF16)],
         [
@@ -992,7 +1020,7 @@
 
     delta_first, inner, *sent = call(
         lower_kernel,
-        [sc, inner, *lower_in, slope_first, skip_inner, backward[0]],
+        [sc, inner, *lower_in, slope_first, skip_inner, forms[1, 0]],
         [fine_tile, fine_grad] + sends(4, 2, 1),
         [
             ((half, low, LANES), F32),
@@ -1029,11 +1057,14 @@
     )
     given = [other_tile(gives[0], 1), other_member(gives[1]), other_both(gives[2], 1)]
     last_in = exchange(*sent)
+    own, last_in[0] = lax.optimization_barrier((own, last_in[0]))
     (total,) = call(adding_kernel, [own, *given], [part(1)], scalars=0, name="chip_sum")
     last_bit = tiles.bit_length() - 2
     for bit in range(2, last_bit + 1):
         if bit == last_bit:
-            total, *last_in = lax.optimization_barrier((total, *last_in))
+            total, last_in[1], last_in[2] = lax.optimization_barrier(
+                (total, last_in[1], last_in[2])
+            )
         given = other_tile(total, bit)
         (total,) = call(adding_kernel, [total, given], [part(1)], scalars=0, name=f"sum_{bit}")
     (derivative,) = call(

time: 128 us -> 122 us (0.953)
  waiting for transfers between devices: 34.4 us -> 27.9 us
  starting transfers between devices: 46.7 us -> 52.5 us
  Pallas kernels: 38 us -> 34.2 us
  local copies, waits for them, and re-layouts: 8.07 us -> 5.86 us
    ppermute x9, waiting for transfers between devices: 10.6 us -> 2.65 us  [other_tile(): return lax.ppermute(array, 'tile', pairs)]
    ppermute x30, waiting for transfers between devices: 16.7 us -> 21.9 us  [shifted(): return lax.ppermute(array, 'tile', pairs)]
    pallas_call x18 -> x19, Pallas kernels: 38 us -> 34.2 us  [call(): pl.pallas_call(body, out_shape=[jax.ShapeDtypeStruct(shape, kind) for sha...]
    ppermute x9, starting transfers between devices: 3.92 us -> 7.17 us  [other_tile(): return lax.ppermute(array, 'tile', pairs)]
    ppermute x2, waiting for transfers between devices: 4.23 us -> 1.81 us  [other_both(): return lax.ppermute(array, ('ens', 'tile'), pairs)]
    unnamed x20 -> x24, local copies, waits for them, and re-layouts: 7.31 us -> 5.07 us
    ppermute x2, starting transfers between devices: 2.41 us -> 3.86 us  [other_both(): return lax.ppermute(array, ('ens', 'tile'), pairs)]
    ppermute x2, waiting for transfers between devices: 2.88 us -> 1.58 us  [other_member(): return lax.ppermute(array, 'ens', [(0, 1), (1, 0)])]
  transfers between devices with their start and end apart: 43 -> 43, of which waited for: 17 -> 17; matrix products, arithmetic and copies ran while one was open for 0% -> 0% of each run, Pallas kernels for 14% -> 13%
where the time goes in v1:
time: 122 us; the launch traced here: 121 us
  starting transfers between devices  52.5 us (43%)
  Pallas kernels  34.2 us (28%)
  waiting for transfers between devices  27.9 us (23%)
  local copies, waits for them, and re-layouts  5.86 us (5%)
    ppermute x30, starting transfers between devices, shifted(): return lax.ppermute(array, 'tile', pairs)  39.4 us
    pallas_call x19, Pallas kernels, call(): pl.pallas_call(body, out_shape=[jax.ShapeDtypeStruct(shape, kind) for sha...  34.2 us
    ppermute x30, waiting for transfers between devices, shifted(): return lax.ppermute(array, 'tile', pairs)  21.9 us
    ppermute x9, starting transfers between devices, other_tile(): return lax.ppermute(array, 'tile', pairs)  7.17 us
    unnamed x24, local copies, waits for them, and re-layouts  5.07 us
    ppermute x2, starting transfers between devices, other_both(): return lax.ppermute(array, ('ens', 'tile'), pairs)  3.86 us
    ppermute x9, waiting for transfers between devices, other_tile(): return lax.ppermute(array, 'tile', pairs)  2.65 us
  transfers between devices with their start and end apart: 43, of which 17 were waited for; matrix products, arithmetic and copies ran while one was open for 0% of the time, Pallas kernels for 13%

profile of v1, /device:TPU:0, one launch (start us, length us, event | category | flops | bytes accessed | tf_op | source)
XLA Modules:
  0.0 121.4 jit_solution(12687467382353510116)
XLA Ops:
  3.3 4.1 %collective-permute-start = (bf16[2,17,16,128]{3,2,1,0:T(8,128)(2,1)S(1)}, bf16[2,17,16,128]{3,2,1,0:T(8,128)(2,1)S(1)}, u32[]{:S(2)}, u32[]{:S(2)}) collective-permute-start(bf16[2,17,16,128]{3,2,1,0:T(8,128)(2,1)S(1)} %get-tuple-element.114), channel_id=1, source_target_pairs={{0,8},{1,9},{2,10},{3,11},{4,12},{5,13},{6,14},{7,15},{8,0},{9,1},... | collective-permute-start | bytes 417800 | tf_op jit(solution)/shard_map/ppermute | solution.py:796
  7.4 2.4 %collective-permute-start.2 = (bf16[2,16,128]{2,1,0:T(8,128)(2,1)S(1)}, bf16[2,16,128]{2,1,0:T(8,128)(2,1)S(1)}, u32[]{:S(2)}, u32[]{:S(2)}) collective-permute-start(bf16[2,16,128]{2,1,0:T(8,128)(2,1)S(1)} %get-tuple-element.116), channel_id=1, source_target_pairs={{0,15},{1,2},{2,1},{3,4},{4,3},{5,6},{6,5},{7,8},{8,7},{9,10},{10,... | collective-permute-start | bytes 24584 | tf_op jit(solution)/shard_map/ppermute | solution.py:796
  14.2 3.8 %first_layer.1 = (bf16[16,64,128]{2,1,0:T(8,128)(2,1)S(1)}, f32[16,64,128]{2,1,0:T(8,128)S(1)}, bf16[8,64,128]{2,1,0:T(8,128)(2,1)S(1)}, s32[13]{0:T(128)S(1)}, ...) custom-call(s32[13]{0:T(128)S(1)} %concatenate.3.sc.own_sc, ...), custom_call_target="tpu_custom_call" | custom-call | flops 150994944 | bytes 2867304 | tf_op jit(solution)/shard_map/first_layer/pallas_call | solution.py:781
  18.0 3.7 %collective-permute-start.5 = (bf16[2,6,64,128]{3,2,1,0:T(8,128)(2,1)S(1)}, bf16[2,6,64,128]{3,2,1,0:T(8,128)(2,1)S(1)}, u32[]{:S(2)}, u32[]{:S(2)}) collective-permute-start(bf16[2,6,64,128]{3,2,1,0:T(8,128)(2,1)S(1)} %get-tuple-element.123), channel_id=1, source_target_pairs={{0,8},{1,9},{2,10},{3,11},{4,12},{5,13},{6,14},{7,15},{8,0},{9,1},... | collective-permute-start | bytes 589832 | tf_op jit(solution)/shard_map/ppermute | solution.py:796
  24.1 1.9 %collective-permute-start.7 = (bf16[3,16,128]{2,1,0:T(8,128)(2,1)S(1)}, bf16[3,16,128]{2,1,0:T(8,128)(2,1)S(1)}, u32[]{:S(2)}, u32[]{:S(2)}) collective-permute-start(bf16[3,16,128]{2,1,0:T(8,128)(2,1)S(1)} %get-tuple-element.125), channel_id=1, source_target_pairs={{0,15},{1,2},{2,1},{3,4},{4,3},{5,6},{6,5},{7,8},{8,7},{9,10},{10,... | collective-permute-start | bytes 36872 | tf_op jit(solution)/shard_map/ppermute | solution.py:796
  27.0 3.9 %cotangent_back.1 = (bf16[16,64,128]{2,1,0:T(8,128)(2,1)S(1)}, f32[8,128,128]{2,1,0:T(8,128)S(1)}, f32[16,64,128]{2,1,0:T(8,128)S(1)}, bf16[2,2,64,128]{3,2,1,0:...) custom-call(s32[13]{0:T(128)S(1)} %get-tuple-element.121.sc, ...), custom_call_target="tpu_custom_call" | custom-call | flops 452984832 | bytes 2048052 | tf_op jit(solution)/shard_map/cotangent_back/pallas_call | solution.py:781
  34.2 2.0 %collective-permute-start.10 = (bf16[2,6,64,128]{3,2,1,0:T(8,128)(2,1)S(1)}, bf16[2,6,64,128]{3,2,1,0:T(8,128)(2,1)S(1)}, u32[]{:S(2)}, u32[]{:S(2)}) collective-permute-start(bf16[2,6,64,128]{3,2,1,0:T(8,128)(2,1)S(1)} %get-tuple-element.136), channel_id=1, source_target_pairs={{0,8},{1,9},{2,10},{3,11},{4,12},{5,13},{6,14},{7,15},{8,0},{9,1},... | collective-permute-start | bytes 589832 | tf_op jit(solution)/shard_map/ppermute | solution.py:796
  40.3 2.1 %collective-permute-done.12.refs_2_ = bf16[4,16,128]{2,1,0:T(8,128)(2,1)S(1)} collective-permute-done((bf16[4,16,128]{2,1,0:T(8,128)(2,1)S(1)}, bf16[4,16,128]{2,1,0:T(8,128)(2,1)S(1)}, u32[]{:S(2)}, u32[]{:S(2)}) %collective-permute-start.12) | collective-permute-done | bytes 16416 | tf_op jit(solution)/shard_map/ppermute | solution.py:796
  42.3 4.9 %collective-permute-done.13.refs_3_ = bf16[1,4,16,128]{3,2,1,0:T(8,128)(2,1)S(1)} collective-permute-done((bf16[1,4,16,128]{3,2,1,0:T(8,128)(2,1)S(1)}, bf16[1,4,16,128]{3,2,1,0:T(8,128)(2,1)S(1)}, u32[]{:S(2)}, u32[]{:S(2)}) %collective-permute-start.13) | collective-permute-done | bytes 16416 | tf_op jit(solution)/shard_map/ppermute | solution.py:796
  47.3 4.0 %third_layer_and_back.1 = (bf16[8,128,128]{2,1,0:T(8,128)(2,1)S(1)}, bf16[8,128,128]{2,1,0:T(8,128)(2,1)S(1)}, f32[8,128,128]{2,1,0:T(8,128)S(1)}, bf16[2,6,64,1...) custom-call(s32[13]{0:T(128)S(1)} %get-tuple-element.121.sc, ...), custom_call_target="tpu_custom_call" | custom-call | flops 603979776 | bytes 3014708 | tf_op jit(solution)/shard_map/third_layer_and_back/pallas_call | solution.py:781
  56.9 2.3 %third_terms.1 = bf16[1152,128]{1,0:T(8,128)(2,1)S(1)} custom-call(s32[13]{0:T(128)S(1)} %get-tuple-element.121.sc, bf16[8,128,128]{2,1,0:T(8,128)(2,1)S(1)} %get-tuple-element.135.tile.second, bf16[8,128,128]{2,1,0:T(8,128)(2,1)S(1)} %get-tuple-element.154.delta.delta_third, bf16[2,6,64,128]{3,2,1,0:T(8,128)(2,1)S(1)} %collective-permute-done.10.refs_0_, ...), custom_call_target="tpu_custom_call" | custom-call | flops 301989888 | bytes 1081396 | tf_op jit(solution)/shard_map/third_terms/pallas_call | solution.py:781
  60.3 4.2 %collective-permute-done.18.refs_3_.refs_8_ = bf16[1,4,16,128]{3,2,1,0:T(8,128)(2,1)S(1)} collective-permute-done((bf16[1,4,16,128]{3,2,1,0:T(8,128)(2,1)S(1)}, bf16[1,4,16,128]{3,2,1,0:T(8,128)(2,1)S(1)}, u32[]{:S(2)}, u32[]{:S(2)}) %collective-permute-start.18) | collective-permute-done | bytes 16416 | tf_op jit(solution)/shard_map/ppermute | solution.py:796
  64.5 2.2 %second_back.1 = (bf16[8,128,128]{2,1,0:T(8,128)(2,1)S(1)}, f32[8,64,128]{2,1,0:T(8,128)S(1)}, bf16[2,6,64,128]{3,2,1,0:T(8,128)(2,1)S(1)}, bf16[3,16,128]{2,1,0...) custom-call(s32[13]{0:T(128)S(1)} %get-tuple-element.121.sc, ...), custom_call_target="tpu_custom_call" | custom-call | flops 150994944 | bytes 2375732 | tf_op jit(solution)/shard_map/second_back/pallas_call | solution.py:781
  71.1 2.5 %collective-permute-start.22 = (bf16[3,16,128]{2,1,0:T(8,128)(2,1)S(1)}, bf16[3,16,128]{2,1,0:T(8,128)(2,1)S(1)}, u32[]{:S(2)}, u32[]{:S(2)}) collective-permute-start(bf16[3,16,128]{2,1,0:T(8,128)(2,1)S(1)} %get-tuple-element.180), channel_id=1, source_target_pairs={{0,15},{1,2},{2,1},{3,4},{4,3},{5,6},{6,5},{7,8},{8,7},{9,10},{10,... | collective-permute-start | bytes 36872 | tf_op jit(solution)/shard_map/ppermute | solution.py:796
  73.6 5.5 %joined_layer_and_terms.1 = (bf16[64,16,128]{2,1,0:T(8,128)(2,1)}, bf16[1536,128]{1,0:T(8,128)(2,1)S(1)}) custom-call(s32[13]{0:T(128)S(1)} %get-tuple-element.121.sc, bf16[8,128,128]{2,1,0:T(8,128)(2,1)S(1)} %get-tuple-element.151.coarse, bf16[16,64,128]{2,1,0:T(8,128)(2,1)S(1)} %get-tuple-element.152.fine, ...), custom_call_target="tpu_custom_call" | custom-call | flops 905969664 | bytes 3506228 | tf_op jit(solution)/shard_map/joined_layer_and_terms/pallas_call | solution.py:781
  79.2 2.7 %first_back.1 = (bf16[16,64,128]{2,1,0:T(8,128)(2,1)S(1)}, f32[16,64,128]{2,1,0:T(8,128)S(1)}, bf16[2,4,64,128]{3,2,1,0:T(8,128)(2,1)S(1)}, bf16[2,16,128]{2,1,0...) custom-call(s32[13]{0:T(128)S(1)} %get-tuple-element.121.sc, ...), custom_call_target="tpu_custom_call" | custom-call | flops 150994944 | bytes 2564148 | tf_op jit(solution)/shard_map/first_back/pallas_call | solution.py:781
  89.4 3.6 %collective-permute-done.26.refs_0_ = bf16[2,4,64,128]{3,2,1,0:T(8,128)(2,1)S(1)} collective-permute-done((bf16[2,4,64,128]{3,2,1,0:T(8,128)(2,1)S(1)}, bf16[2,4,64,128]{3,2,1,0:T(8,128)(2,1)S(1)}, u32[]{:S(2)}, u32[]{:S(2)}) %collective-permute-start.26) | collective-permute-done | bytes 131104 | tf_op jit(solution)/shard_map/ppermute | solution.py:796
  95.6 2.3 %collective-permute-start.32 = (bf16[2,16,128]{2,1,0:T(8,128)(2,1)S(1)}, bf16[2,16,128]{2,1,0:T(8,128)(2,1)S(1)}, u32[]{:S(2)}, u32[]{:S(2)}) collective-permute-start(bf16[2,16,128]{2,1,0:T(8,128)(2,1)S(1)} %get-tuple-element.198), channel_id=1, source_target_pairs={{0,15},{1,2},{2,1},{3,4},{4,3},{5,6},{6,5},{7,8},{8,7},{9,10},{10,... | collective-permute-start | bytes 24584 | tf_op jit(solution)/shard_map/ppermute | solution.py:796
  99.1 2.3 %collective-permute-done.32.refs_2_ = bf16[2,16,128]{2,1,0:T(8,128)(2,1)S(1)} collective-permute-done((bf16[2,16,128]{2,1,0:T(8,128)(2,1)S(1)}, bf16[2,16,128]{2,1,0:T(8,128)(2,1)S(1)}, u32[]{:S(2)}, u32[]{:S(2)}) %collective-permute-start.32) | collective-permute-done | bytes 8224 | tf_op jit(solution)/shard_map/ppermute | solution.py:796
  101.5 2.6 %collective-permute-start.35 = (bf16[1,1,16,128]{3,2,1,0:T(8,128)(2,1)S(1)}, bf16[1,1,16,128]{3,2,1,0:T(8,128)(2,1)S(1)}, u32[]{:S(2)}, u32[]{:S(2)}) collective-permute-start(bf16[1,1,16,128]{3,2,1,0:T(8,128)(2,1)S(1)} %get-tuple-element.205), channel_id=1, source_target_pairs={{0,7},{1,10},{2,9},{3,12},{4,11},{5,14},{6,13},{7,0},{8,15},{9,2},... | collective-permute-start | bytes 12296 | tf_op jit(solution)/shard_map/ppermute | solution.py:796
  104.0 2.0 %collective-permute-done.34.refs_3_ = bf16[1,1,16,128]{3,2,1,0:T(8,128)(2,1)S(1)} collective-permute-done((bf16[1,1,16,128]{3,2,1,0:T(8,128)(2,1)S(1)}, bf16[1,1,16,128]{3,2,1,0:T(8,128)(2,1)S(1)}, u32[]{:S(2)}, u32[]{:S(2)}) %collective-permute-start.34) | collective-permute-done | bytes 4128 | tf_op jit(solution)/shard_map/ppermute | solution.py:796
  108.0 3.3 %collective-permute-start.38 = (bf16[384,128]{1,0:T(8,128)(2,1)S(1)}, bf16[384,128]{1,0:T(8,128)(2,1)S(1)}, u32[]{:S(2)}, u32[]{:S(2)}) collective-permute-start(bf16[384,128]{1,0:T(8,128)(2,1)S(1)} %sum_3.1.refs_0_), channel_id=1, source_target_pairs={{0,18},{1,19},{2,16},{3,17},{4,22},{5,23},{6,20},{7,21},{8,26},{9,... | collective-permute-start | bytes 294920 | tf_op jit(solution)/shard_map/ppermute | solution.py:816
  111.9 2.0 %collective-permute-start.39 = (bf16[384,128]{1,0:T(8,128)(2,1)S(1)}, bf16[384,128]{1,0:T(8,128)(2,1)S(1)}, u32[]{:S(2)}, u32[]{:S(2)}) collective-permute-start(bf16[384,128]{1,0:T(8,128)(2,1)S(1)} %sum_3.1.refs_0_), channel_id=1, source_target_pairs={{0,1},{1,0},{2,3},{3,2},{4,5},{5,4},{6,7},{7,6},{8,9},{9,8},{10,11... | collective-permute-start | bytes 294920 | tf_op jit(solution)/shard_map/ppermute | solution.py:805
  119.4 2.0 %unpack_sums.1 = (f32[9,64,64]{2,1,0:T(8,128)}, f32[9,64,128]{2,1,0:T(8,128)}, f32[9,128,128]{2,1,0:T(8,128)}, f32[9,64,192]{2,1,0:T(8,128)}, f32[1,64]{1,0:T(1,...) custom-call(s32[13]{0:T(128)S(1)} %get-tuple-element.121.sc, bf16[384,128]{1,0:T(8,128)(2,1)S(1)} %sum_3.1.refs_0_, ...), custom_call_target="tpu_custom_call" | custom-call | bytes 2262580 | tf_op jit(solution)/shard_map/unpack_sums/pallas_call | solution.py:781
  (107 shorter events, 48.1 us)
Async XLA Ops:
  3.3 10.9 %collective-permute-start = (bf16[2,17,16,128]{3,2,1,0:T(8,128)(2,1)S(1)}, bf16[2,17,16,128]{3,2,1,0:T(8,128)(2,1)S(1)}, u32[]{:S(2)}, u32[]{:S(2)}) collective-permute-start(bf16[2,17,16,128]{3,2,1,0:T(8,128)(2,1)S(1)} %get-tuple-element.114), channel_id=1, source_target_pairs={{0,8},{1,9},{2,10},{3,11},{4,12},{5,13},{6,14},{7,15},{8,0},{9,1},... | collective-permute-start | bytes 417800 | tf_op jit(solution)/shard_map/ppermute | solution.py:796
  7.4 6.7 %collective-permute-start.1 = (bf16[2,16,128]{2,1,0:T(8,128)(2,1)S(1)}, bf16[2,16,128]{2,1,0:T(8,128)(2,1)S(1)}, u32[]{:S(2)}, u32[]{:S(2)}) collective-permute-start(bf16[2,16,128]{2,1,0:T(8,128)(2,1)S(1)} %get-tuple-element.115), channel_id=1, source_target_pairs={{0,1},{1,0},{2,3},{3,2},{4,5},{5,4},{6,7},{7,6},{8,9},{9,8},{10,11... | collective-permute-start | bytes 24584 | tf_op jit(solution)/shard_map/ppermute | solution.py:796
  7.4 6.7 %collective-permute-start.2 = (bf16[2,16,128]{2,1,0:T(8,128)(2,1)S(1)}, bf16[2,16,128]{2,1,0:T(8,128)(2,1)S(1)}, u32[]{:S(2)}, u32[]{:S(2)}) collective-permute-start(bf16[2,16,128]{2,1,0:T(8,128)(2,1)S(1)} %get-tuple-element.116), channel_id=1, source_target_pairs={{0,15},{1,2},{2,1},{3,4},{4,3},{5,6},{6,5},{7,8},{8,7},{9,10},{10,... | collective-permute-start | bytes 24584 | tf_op jit(solution)/shard_map/ppermute | solution.py:796
  18.0 14.4 %collective-permute-start.5 = (bf16[2,6,64,128]{3,2,1,0:T(8,128)(2,1)S(1)}, bf16[2,6,64,128]{3,2,1,0:T(8,128)(2,1)S(1)}, u32[]{:S(2)}, u32[]{:S(2)}) collective-permute-start(bf16[2,6,64,128]{3,2,1,0:T(8,128)(2,1)S(1)} %get-tuple-element.123), channel_id=1, source_target_pairs={{0,8},{1,9},{2,10},{3,11},{4,12},{5,13},{6,14},{7,15},{8,0},{9,1},... | collective-permute-start | bytes 589832 | tf_op jit(solution)/shard_map/ppermute | solution.py:796
  21.8 10.7 %collective-permute-start.8 = (bf16[1,2,16,128]{3,2,1,0:T(8,128)(2,1)S(1)}, bf16[1,2,16,128]{3,2,1,0:T(8,128)(2,1)S(1)}, u32[]{:S(2)}, u32[]{:S(2)}) collective-permute-start(bf16[1,2,16,128]{3,2,1,0:T(8,128)(2,1)S(1)} %get-tuple-element.126), channel_id=1, source_target_pairs={{0,9},{1,8},{2,11},{3,10},{4,13},{5,12},{6,15},{7,14},{8,1},{9,0},... | collective-permute-start | bytes 24584 | tf_op jit(solution)/shard_map/ppermute | solution.py:796
  22.6 9.8 %collective-permute-start.9 = (bf16[1,2,16,128]{3,2,1,0:T(8,128)(2,1)S(1)}, bf16[1,2,16,128]{3,2,1,0:T(8,128)(2,1)S(1)}, u32[]{:S(2)}, u32[]{:S(2)}) collective-permute-start(bf16[1,2,16,128]{3,2,1,0:T(8,128)(2,1)S(1)} %get-tuple-element.127), channel_id=1, source_target_pairs={{0,7},{1,10},{2,9},{3,12},{4,11},{5,14},{6,13},{7,0},{8,15},{9,2},... | collective-permute-start | bytes 24584 | tf_op jit(solution)/shard_map/ppermute | solution.py:796
  24.1 8.4 %collective-permute-start.6 = (bf16[3,16,128]{2,1,0:T(8,128)(2,1)S(1)}, bf16[3,16,128]{2,1,0:T(8,128)(2,1)S(1)}, u32[]{:S(2)}, u32[]{:S(2)}) collective-permute-start(bf16[3,16,128]{2,1,0:T(8,128)(2,1)S(1)} %get-tuple-element.124), channel_id=1, source_target_pairs={{0,1},{1,0},{2,3},{3,2},{4,5},{5,4},{6,7},{7,6},{8,9},{9,8},{10,11... | collective-permute-start | bytes 36872 | tf_op jit(solution)/shard_map/ppermute | solution.py:796
  24.1 8.4 %collective-permute-start.7 = (bf16[3,16,128]{2,1,0:T(8,128)(2,1)S(1)}, bf16[3,16,128]{2,1,0:T(8,128)(2,1)S(1)}, u32[]{:S(2)}, u32[]{:S(2)}) collective-permute-start(bf16[3,16,128]{2,1,0:T(8,128)(2,1)S(1)} %get-tuple-element.125), channel_id=1, source_target_pairs={{0,15},{1,2},{2,1},{3,4},{4,3},{5,6},{6,5},{7,8},{8,7},{9,10},{10,... | collective-permute-start | bytes 36872 | tf_op jit(solution)/shard_map/ppermute | solution.py:796
  34.2 13.0 %collective-permute-start.10 = (bf16[2,6,64,128]{3,2,1,0:T(8,128)(2,1)S(1)}, bf16[2,6,64,128]{3,2,1,0:T(8,128)(2,1)S(1)}, u32[]{:S(2)}, u32[]{:S(2)}) collective-permute-start(bf16[2,6,64,128]{3,2,1,0:T(8,128)(2,1)S(1)} %get-tuple-element.136), channel_id=1, source_target_pairs={{0,8},{1,9},{2,10},{3,11},{4,12},{5,13},{6,14},{7,15},{8,0},{9,1},... | collective-permute-start | bytes 589832 | tf_op jit(solution)/shard_map/ppermute | solution.py:796
  38.0 9.2 %collective-permute-start.13 = (bf16[1,4,16,128]{3,2,1,0:T(8,128)(2,1)S(1)}, bf16[1,4,16,128]{3,2,1,0:T(8,128)(2,1)S(1)}, u32[]{:S(2)}, u32[]{:S(2)}) collective-permute-start(bf16[1,4,16,128]{3,2,1,0:T(8,128)(2,1)S(1)} %get-tuple-element.139), channel_id=1, source_target_pairs={{0,9},{1,8},{2,11},{3,10},{4,13},{5,12},{6,15},{7,14},{8,1},{9,0},... | collective-permute-start | bytes 49160 | tf_op jit(solution)/shard_map/ppermute | solution.py:796
  38.5 8.8 %collective-permute-start.14 = (bf16[1,4,16,128]{3,2,1,0:T(8,128)(2,1)S(1)}, bf16[1,4,16,128]{3,2,1,0:T(8,128)(2,1)S(1)}, u32[]{:S(2)}, u32[]{:S(2)}) collective-permute-start(bf16[1,4,16,128]{3,2,1,0:T(8,128)(2,1)S(1)} %get-tuple-element.140), channel_id=1, source_target_pairs={{0,7},{1,10},{2,9},{3,12},{4,11},{5,14},{6,13},{7,0},{8,15},{9,2},... | collective-permute-start | bytes 49160 | tf_op jit(solution)/shard_map/ppermute | solution.py:796
  51.2 13.2 %collective-permute-start.15 = (bf16[2,6,64,128]{3,2,1,0:T(8,128)(2,1)S(1)}, bf16[2,6,64,128]{3,2,1,0:T(8,128)(2,1)S(1)}, u32[]{:S(2)}, u32[]{:S(2)}) collective-permute-start(bf16[2,6,64,128]{3,2,1,0:T(8,128)(2,1)S(1)} %get-tuple-element.157), channel_id=1, source_target_pairs={{0,8},{1,9},{2,10},{3,11},{4,12},{5,13},{6,14},{7,15},{8,0},{9,1},... | collective-permute-start | bytes 589832 | tf_op jit(solution)/shard_map/ppermute | solution.py:796
  52.8 7.4 %collective-permute-start.17 = (bf16[4,16,128]{2,1,0:T(8,128)(2,1)S(1)}, bf16[4,16,128]{2,1,0:T(8,128)(2,1)S(1)}, u32[]{:S(2)}, u32[]{:S(2)}) collective-permute-start(bf16[4,16,128]{2,1,0:T(8,128)(2,1)S(1)} %get-tuple-element.159), channel_id=1, source_target_pairs={{0,15},{1,2},{2,1},{3,4},{4,3},{5,6},{6,5},{7,8},{8,7},{9,10},{10,... | collective-permute-start | bytes 49160 | tf_op jit(solution)/shard_map/ppermute | solution.py:796
  54.4 10.0 %collective-permute-start.18 = (bf16[1,4,16,128]{3,2,1,0:T(8,128)(2,1)S(1)}, bf16[1,4,16,128]{3,2,1,0:T(8,128)(2,1)S(1)}, u32[]{:S(2)}, u32[]{:S(2)}) collective-permute-start(bf16[1,4,16,128]{3,2,1,0:T(8,128)(2,1)S(1)} %get-tuple-element.160), channel_id=1, source_target_pairs={{0,9},{1,8},{2,11},{3,10},{4,13},{5,12},{6,15},{7,14},{8,1},{9,0},... | collective-permute-start | bytes 49160 | tf_op jit(solution)/shard_map/ppermute | solution.py:796
  55.8 8.7 %collective-permute-start.19 = (bf16[1,4,16,128]{3,2,1,0:T(8,128)(2,1)S(1)}, bf16[1,4,16,128]{3,2,1,0:T(8,128)(2,1)S(1)}, u32[]{:S(2)}, u32[]{:S(2)}) collective-permute-start(bf16[1,4,16,128]{3,2,1,0:T(8,128)(2,1)S(1)} %get-tuple-element.161), channel_id=1, source_target_pairs={{0,7},{1,10},{2,9},{3,12},{4,11},{5,14},{6,13},{7,0},{8,15},{9,2},... | collective-permute-start | bytes 49160 | tf_op jit(solution)/shard_map/ppermute | solution.py:796
  66.7 12.4 %collective-permute-start.20 = (bf16[2,6,64,128]{3,2,1,0:T(8,128)(2,1)S(1)}, bf16[2,6,64,128]{3,2,1,0:T(8,128)(2,1)S(1)}, u32[]{:S(2)}, u32[]{:S(2)}) collective-permute-start(bf16[2,6,64,128]{3,2,1,0:T(8,128)(2,1)S(1)} %get-tuple-element.176), channel_id=1, source_target_pairs={{0,8},{1,9},{2,10},{3,11},{4,12},{5,13},{6,14},{7,15},{8,0},{9,1},... | collective-permute-start | bytes 589832 | tf_op jit(solution)/shard_map/ppermute | solution.py:796
  68.2 11.0 %collective-permute-start.23 = (bf16[1,2,16,128]{3,2,1,0:T(8,128)(2,1)S(1)}, bf16[1,2,16,128]{3,2,1,0:T(8,128)(2,1)S(1)}, u32[]{:S(2)}, u32[]{:S(2)}) collective-permute-start(bf16[1,2,16,128]{3,2,1,0:T(8,128)(2,1)S(1)} %get-tuple-element.181), channel_id=1, source_target_pairs={{0,9},{1,8},{2,11},{3,10},{4,13},{5,12},{6,15},{7,14},{8,1},{9,0},... | collective-permute-start | bytes 24584 | tf_op jit(solution)/shard_map/ppermute | solution.py:796
  69.6 9.6 %collective-permute-start.24 = (bf16[1,2,16,128]{3,2,1,0:T(8,128)(2,1)S(1)}, bf16[1,2,16,128]{3,2,1,0:T(8,128)(2,1)S(1)}, u32[]{:S(2)}, u32[]{:S(2)}) collective-permute-start(bf16[1,2,16,128]{3,2,1,0:T(8,128)(2,1)S(1)} %get-tuple-element.182), channel_id=1, source_target_pairs={{0,7},{1,10},{2,9},{3,12},{4,11},{5,14},{6,13},{7,0},{8,15},{9,2},... | collective-permute-start | bytes 24584 | tf_op jit(solution)/shard_map/ppermute | solution.py:796
  70.1 9.1 %collective-permute-start.21 = (bf16[3,16,128]{2,1,0:T(8,128)(2,1)S(1)}, bf16[3,16,128]{2,1,0:T(8,128)(2,1)S(1)}, u32[]{:S(2)}, u32[]{:S(2)}) collective-permute-start(bf16[3,16,128]{2,1,0:T(8,128)(2,1)S(1)} %get-tuple-element.179), channel_id=1, source_target_pairs={{0,1},{1,0},{2,3},{3,2},{4,5},{5,4},{6,7},{7,6},{8,9},{9,8},{10,11... | collective-permute-start | bytes 36872 | tf_op jit(solution)/shard_map/ppermute | solution.py:796
  71.1 8.1 %collective-permute-start.22 = (bf16[3,16,128]{2,1,0:T(8,128)(2,1)S(1)}, bf16[3,16,128]{2,1,0:T(8,128)(2,1)S(1)}, u32[]{:S(2)}, u32[]{:S(2)}) collective-permute-start(bf16[3,16,128]{2,1,0:T(8,128)(2,1)S(1)} %get-tuple-element.180), channel_id=1, source_target_pairs={{0,15},{1,2},{2,1},{3,4},{4,3},{5,6},{6,5},{7,8},{8,7},{9,10},{10,... | collective-permute-start | bytes 36872 | tf_op jit(solution)/shard_map/ppermute | solution.py:796
  83.9 9.2 %collective-permute-start.26 = (bf16[2,4,64,128]{3,2,1,0:T(8,128)(2,1)S(1)}, bf16[2,4,64,128]{3,2,1,0:T(8,128)(2,1)S(1)}, u32[]{:S(2)}, u32[]{:S(2)}) collective-permute-start(bf16[2,4,64,128]{3,2,1,0:T(8,128)(2,1)S(1)} %get-tuple-element.192), channel_id=1, source_target_pairs={{0,8},{1,9},{2,10},{3,11},{4,12},{5,13},{6,14},{7,15},{8,0},{9,1},... | collective-permute-start | bytes 393224 | tf_op jit(solution)/shard_map/ppermute | solution.py:796
  85.9 7.2 %collective-permute-start.27 = (bf16[384,128]{1,0:T(8,128)(2,1)S(1)}, bf16[384,128]{1,0:T(8,128)(2,1)S(1)}, u32[]{:S(2)}, u32[]{:S(2)}) collective-permute-start(bf16[384,128]{1,0:T(8,128)(2,1)S(1)} %get-tuple-element.194), channel_id=1, source_target_pairs={{0,2},{1,3},{2,0},{3,1},{4,6},{5,7},{6,4},{7,5},{8,10},{9,11},{10,... | collective-permute-start | bytes 294920 | tf_op jit(solution)/shard_map/ppermute | solution.py:805
  101.4 6.6 %collective-permute-start.33 = (bf16[384,128]{1,0:T(8,128)(2,1)S(1)}, bf16[384,128]{1,0:T(8,128)(2,1)S(1)}, u32[]{:S(2)}, u32[]{:S(2)}) collective-permute-start(bf16[384,128]{1,0:T(8,128)(2,1)S(1)} %sum_2.1.refs_0_), channel_id=1, source_target_pairs={{0,8},{1,9},{2,10},{3,11},{4,12},{5,13},{6,14},{7,15},{8,0},{9,1},... | collective-permute-start | bytes 294920 | tf_op jit(solution)/shard_map/ppermute | solution.py:805
  108.0 6.5 %collective-permute-start.38 = (bf16[384,128]{1,0:T(8,128)(2,1)S(1)}, bf16[384,128]{1,0:T(8,128)(2,1)S(1)}, u32[]{:S(2)}, u32[]{:S(2)}) collective-permute-start(bf16[384,128]{1,0:T(8,128)(2,1)S(1)} %sum_3.1.refs_0_), channel_id=1, source_target_pairs={{0,18},{1,19},{2,16},{3,17},{4,22},{5,23},{6,20},{7,21},{8,26},{9,... | collective-permute-start | bytes 294920 | tf_op jit(solution)/shard_map/ppermute | solution.py:816
  (31 other events, 161.8 us)

commit v2 on v1

--- a/solution.py
+++ b/solution.py
@@ -1057,14 +1057,9 @@
     )
     given = [other_tile(gives[0], 1), other_member(gives[1]), other_both(gives[2], 1)]
     last_in = exchange(*sent)
-    own, last_in[0] = lax.optimization_barrier((own, last_in[0]))
+    own, *last_in[:3] = lax.optimization_barrier((own, *last_in[:3]))
     (total,) = call(adding_kernel, [own, *given], [part(1)], scalars=0, name="chip_sum")
-    last_bit = tiles.bit_length() - 2
-    for bit in range(2, last_bit + 1):
-        if bit == last_bit:
-            total, last_in[1], last_in[2] = lax.optimization_barrier(
-                (total, last_in[1], last_in[2])
-            )
+    for bit in range(2, tiles.bit_length() - 1):
         given = other_tile(total, bit)
         (total,) = call(adding_kernel, [total, given], [part(1)], scalars=0, name=f"sum_{bit}")
     (derivative,) = call(

time: 122 us -> 122 us (level)
    ppermute x9, waiting for transfers between devices: 2.65 us -> 6.29 us  [other_tile(): return lax.ppermute(array, 'tile', pairs)]
    ppermute x30, waiting for transfers between devices: 21.9 us -> 20.1 us  [shifted(): return lax.ppermute(array, 'tile', pairs)]
  transfers between devices with their start and end apart: 43 -> 43, of which waited for: 17 -> 16; matrix products, arithmetic and copies ran while one was open for 0% -> 0% of each run, Pallas kernels for 13% -> 13%
where the time goes in v2:
time: 122 us
  starting transfers between devices  52.1 us (43%)
  Pallas kernels  34.2 us (28%)
  waiting for transfers between devices  28.4 us (23%)
  local copies, waits for them, and re-layouts  5.86 us (5%)
    ppermute x30, starting transfers between devices, shifted(): return lax.ppermute(array, 'tile', pairs)  39.5 us
    pallas_call x19, Pallas kernels, call(): pl.pallas_call(body, out_shape=[jax.ShapeDtypeStruct(shape, kind) for sha...  34.2 us
    ppermute x30, waiting for transfers between devices, shifted(): return lax.ppermute(array, 'tile', pairs)  20.1 us
    ppermute x9, waiting for transfers between devices, other_tile(): return lax.ppermute(array, 'tile', pairs)  6.29 us
    ppermute x9, starting transfers between devices, other_tile(): return lax.ppermute(array, 'tile', pairs)  6.18 us
    unnamed x24, local copies, waits for them, and re-layouts  5.07 us
    ppermute x2, starting transfers between devices, other_both(): return lax.ppermute(array, ('ens', 'tile'), pairs)  4.47 us
  transfers between devices with their start and end apart: 43, of which 16 were waited for; matrix products, arithmetic and copies ran while one was open for 0% of the time, Pallas kernels for 13%

profile of v2, /device:TPU:0, one launch (start us, length us, event | category | flops | bytes accessed | tf_op | source)
XLA Modules:
  0.0 121.5 jit_solution(4952141972020944967)
XLA Ops:
  3.3 4.1 %collective-permute-start = (bf16[2,17,16,128]{3,2,1,0:T(8,128)(2,1)S(1)}, bf16[2,17,16,128]{3,2,1,0:T(8,128)(2,1)S(1)}, u32[]{:S(2)}, u32[]{:S(2)}) collective-permute-start(bf16[2,17,16,128]{3,2,1,0:T(8,128)(2,1)S(1)} %get-tuple-element.113), channel_id=1, source_target_pairs={{0,8},{1,9},{2,10},{3,11},{4,12},{5,13},{6,14},{7,15},{8,0},{9,1},... | collective-permute-start | bytes 417800 | tf_op jit(solution)/shard_map/ppermute | solution.py:796
  7.4 2.4 %collective-permute-start.2 = (bf16[2,16,128]{2,1,0:T(8,128)(2,1)S(1)}, bf16[2,16,128]{2,1,0:T(8,128)(2,1)S(1)}, u32[]{:S(2)}, u32[]{:S(2)}) collective-permute-start(bf16[2,16,128]{2,1,0:T(8,128)(2,1)S(1)} %get-tuple-element.115), channel_id=1, source_target_pairs={{0,15},{1,2},{2,1},{3,4},{4,3},{5,6},{6,5},{7,8},{8,7},{9,10},{10,... | collective-permute-start | bytes 24584 | tf_op jit(solution)/shard_map/ppermute | solution.py:796
  14.2 3.8 %first_layer.1 = (bf16[16,64,128]{2,1,0:T(8,128)(2,1)S(1)}, f32[16,64,128]{2,1,0:T(8,128)S(1)}, bf16[8,64,128]{2,1,0:T(8,128)(2,1)S(1)}, s32[13]{0:T(128)S(1)}, ...) custom-call(s32[13]{0:T(128)S(1)} %concatenate.3.sc.own_sc, ...), custom_call_target="tpu_custom_call" | custom-call | flops 150994944 | bytes 2867304 | tf_op jit(solution)/shard_map/first_layer/pallas_call | solution.py:781
  18.0 3.7 %collective-permute-start.5 = (bf16[2,6,64,128]{3,2,1,0:T(8,128)(2,1)S(1)}, bf16[2,6,64,128]{3,2,1,0:T(8,128)(2,1)S(1)}, u32[]{:S(2)}, u32[]{:S(2)}) collective-permute-start(bf16[2,6,64,128]{3,2,1,0:T(8,128)(2,1)S(1)} %get-tuple-element.122), channel_id=1, source_target_pairs={{0,8},{1,9},{2,10},{3,11},{4,12},{5,13},{6,14},{7,15},{8,0},{9,1},... | collective-permute-start | bytes 589832 | tf_op jit(solution)/shard_map/ppermute | solution.py:796
  24.1 1.9 %collective-permute-start.7 = (bf16[3,16,128]{2,1,0:T(8,128)(2,1)S(1)}, bf16[3,16,128]{2,1,0:T(8,128)(2,1)S(1)}, u32[]{:S(2)}, u32[]{:S(2)}) collective-permute-start(bf16[3,16,128]{2,1,0:T(8,128)(2,1)S(1)} %get-tuple-element.124), channel_id=1, source_target_pairs={{0,15},{1,2},{2,1},{3,4},{4,3},{5,6},{6,5},{7,8},{8,7},{9,10},{10,... | collective-permute-start | bytes 36872 | tf_op jit(solution)/shard_map/ppermute | solution.py:796
  27.0 3.9 %cotangent_back.1 = (bf16[16,64,128]{2,1,0:T(8,128)(2,1)S(1)}, f32[8,128,128]{2,1,0:T(8,128)S(1)}, f32[16,64,128]{2,1,0:T(8,128)S(1)}, bf16[2,2,64,128]{3,2,1,0:...) custom-call(s32[13]{0:T(128)S(1)} %get-tuple-element.120.sc, ...), custom_call_target="tpu_custom_call" | custom-call | flops 452984832 | bytes 2048052 | tf_op jit(solution)/shard_map/cotangent_back/pallas_call | solution.py:781
  34.2 2.0 %collective-permute-start.10 = (bf16[2,6,64,128]{3,2,1,0:T(8,128)(2,1)S(1)}, bf16[2,6,64,128]{3,2,1,0:T(8,128)(2,1)S(1)}, u32[]{:S(2)}, u32[]{:S(2)}) collective-permute-start(bf16[2,6,64,128]{3,2,1,0:T(8,128)(2,1)S(1)} %get-tuple-element.135), channel_id=1, source_target_pairs={{0,8},{1,9},{2,10},{3,11},{4,12},{5,13},{6,14},{7,15},{8,0},{9,1},... | collective-permute-start | bytes 589832 | tf_op jit(solution)/shard_map/ppermute | solution.py:796
  36.2 1.8 %collective-permute-start.12 = (bf16[4,16,128]{2,1,0:T(8,128)(2,1)S(1)}, bf16[4,16,128]{2,1,0:T(8,128)(2,1)S(1)}, u32[]{:S(2)}, u32[]{:S(2)}) collective-permute-start(bf16[4,16,128]{2,1,0:T(8,128)(2,1)S(1)} %get-tuple-element.137), channel_id=1, source_target_pairs={{0,15},{1,2},{2,1},{3,4},{4,3},{5,6},{6,5},{7,8},{8,7},{9,10},{10,... | collective-permute-start | bytes 49160 | tf_op jit(solution)/shard_map/ppermute | solution.py:796
  40.3 2.1 %collective-permute-done.12.refs_2_ = bf16[4,16,128]{2,1,0:T(8,128)(2,1)S(1)} collective-permute-done((bf16[4,16,128]{2,1,0:T(8,128)(2,1)S(1)}, bf16[4,16,128]{2,1,0:T(8,128)(2,1)S(1)}, u32[]{:S(2)}, u32[]{:S(2)}) %collective-permute-start.12) | collective-permute-done | bytes 16416 | tf_op jit(solution)/shard_map/ppermute | solution.py:796
  42.3 4.9 %collective-permute-done.13.refs_3_ = bf16[1,4,16,128]{3,2,1,0:T(8,128)(2,1)S(1)} collective-permute-done((bf16[1,4,16,128]{3,2,1,0:T(8,128)(2,1)S(1)}, bf16[1,4,16,128]{3,2,1,0:T(8,128)(2,1)S(1)}, u32[]{:S(2)}, u32[]{:S(2)}) %collective-permute-start.13) | collective-permute-done | bytes 16416 | tf_op jit(solution)/shard_map/ppermute | solution.py:796
  47.3 4.0 %third_layer_and_back.1 = (bf16[8,128,128]{2,1,0:T(8,128)(2,1)S(1)}, bf16[8,128,128]{2,1,0:T(8,128)(2,1)S(1)}, f32[8,128,128]{2,1,0:T(8,128)S(1)}, bf16[2,6,64,1...) custom-call(s32[13]{0:T(128)S(1)} %get-tuple-element.120.sc, ...), custom_call_target="tpu_custom_call" | custom-call | flops 603979776 | bytes 3014708 | tf_op jit(solution)/shard_map/third_layer_and_back/pallas_call | solution.py:781
  56.9 2.3 %third_terms.1 = bf16[1152,128]{1,0:T(8,128)(2,1)S(1)} custom-call(s32[13]{0:T(128)S(1)} %get-tuple-element.120.sc, bf16[8,128,128]{2,1,0:T(8,128)(2,1)S(1)} %get-tuple-element.134.tile.second, bf16[8,128,128]{2,1,0:T(8,128)(2,1)S(1)} %get-tuple-element.153.delta.delta_third, bf16[2,6,64,128]{3,2,1,0:T(8,128)(2,1)S(1)} %collective-permute-done.10.refs_0_, ...), custom_call_target="tpu_custom_call" | custom-call | flops 301989888 | bytes 1081396 | tf_op jit(solution)/shard_map/third_terms/pallas_call | solution.py:781
  60.3 4.2 %collective-permute-done.18.refs_3_.refs_8_ = bf16[1,4,16,128]{3,2,1,0:T(8,128)(2,1)S(1)} collective-permute-done((bf16[1,4,16,128]{3,2,1,0:T(8,128)(2,1)S(1)}, bf16[1,4,16,128]{3,2,1,0:T(8,128)(2,1)S(1)}, u32[]{:S(2)}, u32[]{:S(2)}) %collective-permute-start.18) | collective-permute-done | bytes 16416 | tf_op jit(solution)/shard_map/ppermute | solution.py:796
  64.5 2.2 %second_back.1 = (bf16[8,128,128]{2,1,0:T(8,128)(2,1)S(1)}, f32[8,64,128]{2,1,0:T(8,128)S(1)}, bf16[2,6,64,128]{3,2,1,0:T(8,128)(2,1)S(1)}, bf16[3,16,128]{2,1,0...) custom-call(s32[13]{0:T(128)S(1)} %get-tuple-element.120.sc, ...), custom_call_target="tpu_custom_call" | custom-call | flops 150994944 | bytes 2375732 | tf_op jit(solution)/shard_map/second_back/pallas_call | solution.py:781
  71.1 2.6 %collective-permute-start.22 = (bf16[3,16,128]{2,1,0:T(8,128)(2,1)S(1)}, bf16[3,16,128]{2,1,0:T(8,128)(2,1)S(1)}, u32[]{:S(2)}, u32[]{:S(2)}) collective-permute-start(bf16[3,16,128]{2,1,0:T(8,128)(2,1)S(1)} %get-tuple-element.179), channel_id=1, source_target_pairs={{0,15},{1,2},{2,1},{3,4},{4,3},{5,6},{6,5},{7,8},{8,7},{9,10},{10,... | collective-permute-start | bytes 36872 | tf_op jit(solution)/shard_map/ppermute | solution.py:796
  73.6 5.5 %joined_layer_and_terms.1 = (bf16[64,16,128]{2,1,0:T(8,128)(2,1)}, bf16[1536,128]{1,0:T(8,128)(2,1)S(1)}) custom-call(s32[13]{0:T(128)S(1)} %get-tuple-element.120.sc, bf16[8,128,128]{2,1,0:T(8,128)(2,1)S(1)} %get-tuple-element.150.coarse, bf16[16,64,128]{2,1,0:T(8,128)(2,1)S(1)} %get-tuple-element.151.fine, ...), custom_call_target="tpu_custom_call" | custom-call | flops 905969664 | bytes 3506228 | tf_op jit(solution)/shard_map/joined_layer_and_terms/pallas_call | solution.py:781
  79.2 2.7 %first_back.1 = (bf16[16,64,128]{2,1,0:T(8,128)(2,1)S(1)}, f32[16,64,128]{2,1,0:T(8,128)S(1)}, bf16[2,4,64,128]{3,2,1,0:T(8,128)(2,1)S(1)}, bf16[2,16,128]{2,1,0...) custom-call(s32[13]{0:T(128)S(1)} %get-tuple-element.120.sc, ...), custom_call_target="tpu_custom_call" | custom-call | flops 150994944 | bytes 2564148 | tf_op jit(solution)/shard_map/first_back/pallas_call | solution.py:781
  90.6 2.4 %collective-permute-start.28 = (bf16[2,16,128]{2,1,0:T(8,128)(2,1)S(1)}, bf16[2,16,128]{2,1,0:T(8,128)(2,1)S(1)}, u32[]{:S(2)}, u32[]{:S(2)}) collective-permute-start(bf16[2,16,128]{2,1,0:T(8,128)(2,1)S(1)} %get-tuple-element.193), channel_id=1, source_target_pairs={{0,15},{1,2},{2,1},{3,4},{4,3},{5,6},{6,5},{7,8},{8,7},{9,10},{10,... | collective-permute-start | bytes 24584 | tf_op jit(solution)/shard_map/ppermute | solution.py:796
  93.0 3.3 %collective-permute-done.28.refs_2_ = bf16[2,16,128]{2,1,0:T(8,128)(2,1)S(1)} collective-permute-done((bf16[2,16,128]{2,1,0:T(8,128)(2,1)S(1)}, bf16[2,16,128]{2,1,0:T(8,128)(2,1)S(1)}, u32[]{:S(2)}, u32[]{:S(2)}) %collective-permute-start.28) | collective-permute-done | bytes 8224 | tf_op jit(solution)/shard_map/ppermute | solution.py:796
  96.5 4.6 %collective-permute-done.32.refs_1_ = bf16[384,128]{1,0:T(8,128)(2,1)S(1)} collective-permute-done((bf16[384,128]{1,0:T(8,128)(2,1)S(1)}, bf16[384,128]{1,0:T(8,128)(2,1)S(1)}, u32[]{:S(2)}, u32[]{:S(2)}) %collective-permute-start.32) | collective-permute-done | bytes 98336 | tf_op jit(solution)/shard_map/ppermute | solution.py:805
  101.3 2.6 %collective-permute-start.35 = (bf16[1,1,16,128]{3,2,1,0:T(8,128)(2,1)S(1)}, bf16[1,1,16,128]{3,2,1,0:T(8,128)(2,1)S(1)}, u32[]{:S(2)}, u32[]{:S(2)}) collective-permute-start(bf16[1,1,16,128]{3,2,1,0:T(8,128)(2,1)S(1)} %get-tuple-element.203), channel_id=1, source_target_pairs={{0,7},{1,10},{2,9},{3,12},{4,11},{5,14},{6,13},{7,0},{8,15},{9,2},... | collective-permute-start | bytes 12296 | tf_op jit(solution)/shard_map/ppermute | solution.py:796
  105.7 1.9 %last_fold.1 = f32[64,16,128]{2,1,0:T(8,128)} custom-call(s32[13]{0:T(128)S(1)} %get-tuple-element.120.sc, f32[16,64,128]{2,1,0:T(8,128)S(1)} %get-tuple-element.198.inner, bf16[2,4,64,128]{3,2,1,0:T(8,128)(2,1)S(1)} %collective-permute-done.26.refs_0_, bf16[2,16,128]{2,1,0:T(8,128)(2,1)S(1)} %collective-permute-done.27.refs_1_, ...), custom_call_target="tpu_custom_call" | custom-call | bytes 1204276 | tf_op jit(solution)/shard_map/last_fold/pallas_call | solution.py:781
  107.6 3.9 %collective-permute-start.38 = (bf16[384,128]{1,0:T(8,128)(2,1)S(1)}, bf16[384,128]{1,0:T(8,128)(2,1)S(1)}, u32[]{:S(2)}, u32[]{:S(2)}) collective-permute-start(bf16[384,128]{1,0:T(8,128)(2,1)S(1)} %sum_3.1.refs_0_), channel_id=1, source_target_pairs={{0,18},{1,19},{2,16},{3,17},{4,22},{5,23},{6,20},{7,21},{8,26},{9,... | collective-permute-start | bytes 294920 | tf_op jit(solution)/shard_map/ppermute | solution.py:816
  119.5 2.0 %unpack_sums.1 = (f32[9,64,64]{2,1,0:T(8,128)}, f32[9,64,128]{2,1,0:T(8,128)}, f32[9,128,128]{2,1,0:T(8,128)}, f32[9,64,192]{2,1,0:T(8,128)}, f32[1,64]{1,0:T(1,...) custom-call(s32[13]{0:T(128)S(1)} %get-tuple-element.120.sc, bf16[384,128]{1,0:T(8,128)(2,1)S(1)} %sum_3.1.refs_0_, ...), custom_call_target="tpu_custom_call" | custom-call | bytes 2262580 | tf_op jit(solution)/shard_map/unpack_sums/pallas_call | solution.py:781
  (107 shorter events, 45.7 us)
Async XLA Ops:
  3.3 10.9 %collective-permute-start = (bf16[2,17,16,128]{3,2,1,0:T(8,128)(2,1)S(1)}, bf16[2,17,16,128]{3,2,1,0:T(8,128)(2,1)S(1)}, u32[]{:S(2)}, u32[]{:S(2)}) collective-permute-start(bf16[2,17,16,128]{3,2,1,0:T(8,128)(2,1)S(1)} %get-tuple-element.113), channel_id=1, source_target_pairs={{0,8},{1,9},{2,10},{3,11},{4,12},{5,13},{6,14},{7,15},{8,0},{9,1},... | collective-permute-start | bytes 417800 | tf_op jit(solution)/shard_map/ppermute | solution.py:796
  7.4 6.7 %collective-permute-start.2 = (bf16[2,16,128]{2,1,0:T(8,128)(2,1)S(1)}, bf16[2,16,128]{2,1,0:T(8,128)(2,1)S(1)}, u32[]{:S(2)}, u32[]{:S(2)}) collective-permute-start(bf16[2,16,128]{2,1,0:T(8,128)(2,1)S(1)} %get-tuple-element.115), channel_id=1, source_target_pairs={{0,15},{1,2},{2,1},{3,4},{4,3},{5,6},{6,5},{7,8},{8,7},{9,10},{10,... | collective-permute-start | bytes 24584 | tf_op jit(solution)/shard_map/ppermute | solution.py:796
  18.0 14.4 %collective-permute-start.5 = (bf16[2,6,64,128]{3,2,1,0:T(8,128)(2,1)S(1)}, bf16[2,6,64,128]{3,2,1,0:T(8,128)(2,1)S(1)}, u32[]{:S(2)}, u32[]{:S(2)}) collective-permute-start(bf16[2,6,64,128]{3,2,1,0:T(8,128)(2,1)S(1)} %get-tuple-element.122), channel_id=1, source_target_pairs={{0,8},{1,9},{2,10},{3,11},{4,12},{5,13},{6,14},{7,15},{8,0},{9,1},... | collective-permute-start | bytes 589832 | tf_op jit(solution)/shard_map/ppermute | solution.py:796
  21.8 10.7 %collective-permute-start.8 = (bf16[1,2,16,128]{3,2,1,0:T(8,128)(2,1)S(1)}, bf16[1,2,16,128]{3,2,1,0:T(8,128)(2,1)S(1)}, u32[]{:S(2)}, u32[]{:S(2)}) collective-permute-start(bf16[1,2,16,128]{3,2,1,0:T(8,128)(2,1)S(1)} %get-tuple-element.125), channel_id=1, source_target_pairs={{0,9},{1,8},{2,11},{3,10},{4,13},{5,12},{6,15},{7,14},{8,1},{9,0},... | collective-permute-start | bytes 24584 | tf_op jit(solution)/shard_map/ppermute | solution.py:796
  22.6 9.8 %collective-permute-start.9 = (bf16[1,2,16,128]{3,2,1,0:T(8,128)(2,1)S(1)}, bf16[1,2,16,128]{3,2,1,0:T(8,128)(2,1)S(1)}, u32[]{:S(2)}, u32[]{:S(2)}) collective-permute-start(bf16[1,2,16,128]{3,2,1,0:T(8,128)(2,1)S(1)} %get-tuple-element.126), channel_id=1, source_target_pairs={{0,7},{1,10},{2,9},{3,12},{4,11},{5,14},{6,13},{7,0},{8,15},{9,2},... | collective-permute-start | bytes 24584 | tf_op jit(solution)/shard_map/ppermute | solution.py:796
  24.1 8.4 %collective-permute-start.6 = (bf16[3,16,128]{2,1,0:T(8,128)(2,1)S(1)}, bf16[3,16,128]{2,1,0:T(8,128)(2,1)S(1)}, u32[]{:S(2)}, u32[]{:S(2)}) collective-permute-start(bf16[3,16,128]{2,1,0:T(8,128)(2,1)S(1)} %get-tuple-element.123), channel_id=1, source_target_pairs={{0,1},{1,0},{2,3},{3,2},{4,5},{5,4},{6,7},{7,6},{8,9},{9,8},{10,11... | collective-permute-start | bytes 36872 | tf_op jit(solution)/shard_map/ppermute | solution.py:796
  24.1 8.4 %collective-permute-start.7 = (bf16[3,16,128]{2,1,0:T(8,128)(2,1)S(1)}, bf16[3,16,128]{2,1,0:T(8,128)(2,1)S(1)}, u32[]{:S(2)}, u32[]{:S(2)}) collective-permute-start(bf16[3,16,128]{2,1,0:T(8,128)(2,1)S(1)} %get-tuple-element.124), channel_id=1, source_target_pairs={{0,15},{1,2},{2,1},{3,4},{4,3},{5,6},{6,5},{7,8},{8,7},{9,10},{10,... | collective-permute-start | bytes 36872 | tf_op jit(solution)/shard_map/ppermute | solution.py:796
  34.2 13.0 %collective-permute-start.10 = (bf16[2,6,64,128]{3,2,1,0:T(8,128)(2,1)S(1)}, bf16[2,6,64,128]{3,2,1,0:T(8,128)(2,1)S(1)}, u32[]{:S(2)}, u32[]{:S(2)}) collective-permute-start(bf16[2,6,64,128]{3,2,1,0:T(8,128)(2,1)S(1)} %get-tuple-element.135), channel_id=1, source_target_pairs={{0,8},{1,9},{2,10},{3,11},{4,12},{5,13},{6,14},{7,15},{8,0},{9,1},... | collective-permute-start | bytes 589832 | tf_op jit(solution)/shard_map/ppermute | solution.py:796
  38.0 9.2 %collective-permute-start.13 = (bf16[1,4,16,128]{3,2,1,0:T(8,128)(2,1)S(1)}, bf16[1,4,16,128]{3,2,1,0:T(8,128)(2,1)S(1)}, u32[]{:S(2)}, u32[]{:S(2)}) collective-permute-start(bf16[1,4,16,128]{3,2,1,0:T(8,128)(2,1)S(1)} %get-tuple-element.138), channel_id=1, source_target_pairs={{0,9},{1,8},{2,11},{3,10},{4,13},{5,12},{6,15},{7,14},{8,1},{9,0},... | collective-permute-start | bytes 49160 | tf_op jit(solution)/shard_map/ppermute | solution.py:796
  38.5 8.8 %collective-permute-start.14 = (bf16[1,4,16,128]{3,2,1,0:T(8,128)(2,1)S(1)}, bf16[1,4,16,128]{3,2,1,0:T(8,128)(2,1)S(1)}, u32[]{:S(2)}, u32[]{:S(2)}) collective-permute-start(bf16[1,4,16,128]{3,2,1,0:T(8,128)(2,1)S(1)} %get-tuple-element.139), channel_id=1, source_target_pairs={{0,7},{1,10},{2,9},{3,12},{4,11},{5,14},{6,13},{7,0},{8,15},{9,2},... | collective-permute-start | bytes 49160 | tf_op jit(solution)/shard_map/ppermute | solution.py:796
  51.2 13.2 %collective-permute-start.15 = (bf16[2,6,64,128]{3,2,1,0:T(8,128)(2,1)S(1)}, bf16[2,6,64,128]{3,2,1,0:T(8,128)(2,1)S(1)}, u32[]{:S(2)}, u32[]{:S(2)}) collective-permute-start(bf16[2,6,64,128]{3,2,1,0:T(8,128)(2,1)S(1)} %get-tuple-element.156), channel_id=1, source_target_pairs={{0,8},{1,9},{2,10},{3,11},{4,12},{5,13},{6,14},{7,15},{8,0},{9,1},... | collective-permute-start | bytes 589832 | tf_op jit(solution)/shard_map/ppermute | solution.py:796
  52.8 7.4 %collective-permute-start.17 = (bf16[4,16,128]{2,1,0:T(8,128)(2,1)S(1)}, bf16[4,16,128]{2,1,0:T(8,128)(2,1)S(1)}, u32[]{:S(2)}, u32[]{:S(2)}) collective-permute-start(bf16[4,16,128]{2,1,0:T(8,128)(2,1)S(1)} %get-tuple-element.158), channel_id=1, source_target_pairs={{0,15},{1,2},{2,1},{3,4},{4,3},{5,6},{6,5},{7,8},{8,7},{9,10},{10,... | collective-permute-start | bytes 49160 | tf_op jit(solution)/shard_map/ppermute | solution.py:796
  54.4 10.0 %collective-permute-start.18 = (bf16[1,4,16,128]{3,2,1,0:T(8,128)(2,1)S(1)}, bf16[1,4,16,128]{3,2,1,0:T(8,128)(2,1)S(1)}, u32[]{:S(2)}, u32[]{:S(2)}) collective-permute-start(bf16[1,4,16,128]{3,2,1,0:T(8,128)(2,1)S(1)} %get-tuple-element.159), channel_id=1, source_target_pairs={{0,9},{1,8},{2,11},{3,10},{4,13},{5,12},{6,15},{7,14},{8,1},{9,0},... | collective-permute-start | bytes 49160 | tf_op jit(solution)/shard_map/ppermute | solution.py:796
  55.8 8.7 %collective-permute-start.19 = (bf16[1,4,16,128]{3,2,1,0:T(8,128)(2,1)S(1)}, bf16[1,4,16,128]{3,2,1,0:T(8,128)(2,1)S(1)}, u32[]{:S(2)}, u32[]{:S(2)}) collective-permute-start(bf16[1,4,16,128]{3,2,1,0:T(8,128)(2,1)S(1)} %get-tuple-element.160), channel_id=1, source_target_pairs={{0,7},{1,10},{2,9},{3,12},{4,11},{5,14},{6,13},{7,0},{8,15},{9,2},... | collective-permute-start | bytes 49160 | tf_op jit(solution)/shard_map/ppermute | solution.py:796
  66.7 12.4 %collective-permute-start.20 = (bf16[2,6,64,128]{3,2,1,0:T(8,128)(2,1)S(1)}, bf16[2,6,64,128]{3,2,1,0:T(8,128)(2,1)S(1)}, u32[]{:S(2)}, u32[]{:S(2)}) collective-permute-start(bf16[2,6,64,128]{3,2,1,0:T(8,128)(2,1)S(1)} %get-tuple-element.175), channel_id=1, source_target_pairs={{0,8},{1,9},{2,10},{3,11},{4,12},{5,13},{6,14},{7,15},{8,0},{9,1},... | collective-permute-start | bytes 589832 | tf_op jit(solution)/shard_map/ppermute | solution.py:796
  68.2 11.0 %collective-permute-start.23 = (bf16[1,2,16,128]{3,2,1,0:T(8,128)(2,1)S(1)}, bf16[1,2,16,128]{3,2,1,0:T(8,128)(2,1)S(1)}, u32[]{:S(2)}, u32[]{:S(2)}) collective-permute-start(bf16[1,2,16,128]{3,2,1,0:T(8,128)(2,1)S(1)} %get-tuple-element.180), channel_id=1, source_target_pairs={{0,9},{1,8},{2,11},{3,10},{4,13},{5,12},{6,15},{7,14},{8,1},{9,0},... | collective-permute-start | bytes 24584 | tf_op jit(solution)/shard_map/ppermute | solution.py:796
  69.6 9.6 %collective-permute-start.24 = (bf16[1,2,16,128]{3,2,1,0:T(8,128)(2,1)S(1)}, bf16[1,2,16,128]{3,2,1,0:T(8,128)(2,1)S(1)}, u32[]{:S(2)}, u32[]{:S(2)}) collective-permute-start(bf16[1,2,16,128]{3,2,1,0:T(8,128)(2,1)S(1)} %get-tuple-element.181), channel_id=1, source_target_pairs={{0,7},{1,10},{2,9},{3,12},{4,11},{5,14},{6,13},{7,0},{8,15},{9,2},... | collective-permute-start | bytes 24584 | tf_op jit(solution)/shard_map/ppermute | solution.py:796
  70.1 9.1 %collective-permute-start.21 = (bf16[3,16,128]{2,1,0:T(8,128)(2,1)S(1)}, bf16[3,16,128]{2,1,0:T(8,128)(2,1)S(1)}, u32[]{:S(2)}, u32[]{:S(2)}) collective-permute-start(bf16[3,16,128]{2,1,0:T(8,128)(2,1)S(1)} %get-tuple-element.178), channel_id=1, source_target_pairs={{0,1},{1,0},{2,3},{3,2},{4,5},{5,4},{6,7},{7,6},{8,9},{9,8},{10,11... | collective-permute-start | bytes 36872 | tf_op jit(solution)/shard_map/ppermute | solution.py:796
  71.1 8.1 %collective-permute-start.22 = (bf16[3,16,128]{2,1,0:T(8,128)(2,1)S(1)}, bf16[3,16,128]{2,1,0:T(8,128)(2,1)S(1)}, u32[]{:S(2)}, u32[]{:S(2)}) collective-permute-start(bf16[3,16,128]{2,1,0:T(8,128)(2,1)S(1)} %get-tuple-element.179), channel_id=1, source_target_pairs={{0,15},{1,2},{2,1},{3,4},{4,3},{5,6},{6,5},{7,8},{8,7},{9,10},{10,... | collective-permute-start | bytes 36872 | tf_op jit(solution)/shard_map/ppermute | solution.py:796
  83.9 12.5 %collective-permute-start.26 = (bf16[2,4,64,128]{3,2,1,0:T(8,128)(2,1)S(1)}, bf16[2,4,64,128]{3,2,1,0:T(8,128)(2,1)S(1)}, u32[]{:S(2)}, u32[]{:S(2)}) collective-permute-start(bf16[2,4,64,128]{3,2,1,0:T(8,128)(2,1)S(1)} %get-tuple-element.191), channel_id=1, source_target_pairs={{0,8},{1,9},{2,10},{3,11},{4,12},{5,13},{6,14},{7,15},{8,0},{9,1},... | collective-permute-start | bytes 393224 | tf_op jit(solution)/shard_map/ppermute | solution.py:796
  85.9 10.5 %collective-permute-start.29 = (bf16[384,128]{1,0:T(8,128)(2,1)S(1)}, bf16[384,128]{1,0:T(8,128)(2,1)S(1)}, u32[]{:S(2)}, u32[]{:S(2)}) collective-permute-start(bf16[384,128]{1,0:T(8,128)(2,1)S(1)} %get-tuple-element.195), channel_id=1, source_target_pairs={{0,2},{1,3},{2,0},{3,1},{4,6},{5,7},{6,4},{7,5},{8,10},{9,11},{10,... | collective-permute-start | bytes 294920 | tf_op jit(solution)/shard_map/ppermute | solution.py:805
  87.3 9.0 %collective-permute-start.30 = (bf16[384,128]{1,0:T(8,128)(2,1)S(1)}, bf16[384,128]{1,0:T(8,128)(2,1)S(1)}, u32[]{:S(2)}, u32[]{:S(2)}) collective-permute-start(bf16[384,128]{1,0:T(8,128)(2,1)S(1)} %get-tuple-element.196), channel_id=1, source_target_pairs={{0,16},{16,0},{1,17},{17,1},{2,18},{18,2},{3,19},{19,3},{4,20},{20... | collective-permute-start | bytes 294920 | tf_op jit(solution)/shard_map/ppermute | solution.py:809
  88.8 7.6 %collective-permute-start.31 = (bf16[384,128]{1,0:T(8,128)(2,1)S(1)}, bf16[384,128]{1,0:T(8,128)(2,1)S(1)}, u32[]{:S(2)}, u32[]{:S(2)}) collective-permute-start(bf16[384,128]{1,0:T(8,128)(2,1)S(1)} %get-tuple-element.197), channel_id=1, source_target_pairs={{0,18},{1,19},{2,16},{3,17},{4,22},{5,23},{6,20},{7,21},{8,26},{9,... | collective-permute-start | bytes 294920 | tf_op jit(solution)/shard_map/ppermute | solution.py:816
  107.6 6.8 %collective-permute-start.38 = (bf16[384,128]{1,0:T(8,128)(2,1)S(1)}, bf16[384,128]{1,0:T(8,128)(2,1)S(1)}, u32[]{:S(2)}, u32[]{:S(2)}) collective-permute-start(bf16[384,128]{1,0:T(8,128)(2,1)S(1)} %sum_3.1.refs_0_), channel_id=1, source_target_pairs={{0,18},{1,19},{2,16},{3,17},{4,22},{5,23},{6,20},{7,21},{8,26},{9,... | collective-permute-start | bytes 294920 | tf_op jit(solution)/shard_map/ppermute | solution.py:816
  (31 other events, 160.5 us)
